TPU v7x, 128 devices: a whole 4x4x4 slice. The times are simulated.
128 devices in a mesh: dp: 2 (over core), ctx: 64 (over z, y, x).
Axes of the slice: x: 4, y: 4, z: 4, core: 2. Of those that a mesh axis runs over, the one named last changes fastest.
Arguments:
- layer_in: bfloat16 [2, 8192, 576], P('dp', 'ctx'), may hold values from -6 to 6
- positions: int32 [2, 8192], P('dp', 'ctx'), may hold values from 0 to 24575, as said below
- norm_gain1: bfloat16 [576], P('dp'), may hold values from 0.25 to 1.75
- w_query: bfloat16 [576, 576], P('dp'), may hold values from -0.25 to 0.25
- w_key: bfloat16 [576, 192], P('dp'), may hold values from -0.25 to 0.25
- w_value: bfloat16 [576, 192], P('dp'), may hold values from -0.25 to 0.25
- w_out: bfloat16 [576, 576], P('dp'), may hold values from -1.5 to 1.5
- norm_gain2: bfloat16 [576], P('dp'), may hold values from 0.25 to 1.75
- w_gate: bfloat16 [576, 1536], P('dp'), may hold values from -0.25 to 0.25
- w_up: bfloat16 [576, 1536], P('dp'), may hold values from -0.25 to 0.25
- w_down: bfloat16 [1536, 576], P('dp'), may hold values from -0.15625 to 0.15625
- cotangent: bfloat16 [2, 8192, 576], P('dp', 'ctx'), may hold values from -6 to 6
Outputs:
- layer_out: bfloat16 [2, 8192, 576], P('dp', 'ctx')
- input_grad: bfloat16 [2, 8192, 576], P('dp', 'ctx')
- grad_gain1: float32 [576], P('dp')
- grad_query: float32 [576, 576], P('dp')
- grad_key: float32 [576, 192], P('dp')
- grad_value: float32 [576, 192], P('dp')
- grad_out: float32 [576, 576], P('dp')
- grad_gain2: float32 [576], P('dp')
- grad_gate: float32 [576, 1536], P('dp')
- grad_up: float32 [576, 1536], P('dp')
- grad_down: float32 [1536, 576], P('dp')
Inputs may be any that keep to these rules, and one draw needn't show every extreme that they name: Along each sequence the positions rise by 1 or 2 from one token to the next.
All inputs are finite; a program needn't handle non-finite values.
Results may differ from a plain program's by a relative error of at most 0.022.
Values may be sent and summed in bfloat16 or wider, within the bound.
A program may use at most 128 MiB of HBM per device.

v0:
```python
import jax
import jax.numpy as jnp
from jax import lax
from jax.sharding import PartitionSpec as P

HEADS = 9
KV_HEADS = 3
HEAD = 64


EPS = 1e-05
MASKED = -1e30
KEY_BLOCK = 512


def in_one_piece(arrays, axis, dim, along):
    both = jnp.concatenate(arrays, axis=along)
    filled, at, gathered = (lax.all_gather(both, axis, axis=dim, tiled=True), 0, [])
    for a in arrays:
        gathered.append(lax.slice_in_dim(filled, at, at + a.shape[along], axis=along))
        at += a.shape[along]
    return tuple(gathered)


def sent_together(arrays, axis, dim, along):
    both = jnp.concatenate(arrays, axis=along)
    filled, at, gathered = (lax.psum_scatter(both, axis, scatter_dimension=dim, tiled=True), 0, [])
    for a in arrays:
        gathered.append(lax.slice_in_dim(filled, at, at + a.shape[along], axis=along))
        at += a.shape[along]
    return tuple(gathered)


def in_one_piece_2(arrays, axis, dim, along):
    columns = [a.reshape(*a.shape[:along], -1) for a in arrays]
    both = jnp.concatenate(columns, axis=along)
    filled, at, gathered = (lax.all_gather(both, axis, axis=dim, tiled=True), 0, [])
    for a, column in zip(arrays, columns):
        piece = filled[..., at : at + column.shape[along]]
        gathered.append(piece.reshape(*piece.shape[:along], *a.shape[along:]))
        at += column.shape[along]
    return tuple(gathered)


def cut_along(value, dim, devices):
    lengths = value.shape
    blocks = value.reshape(*lengths[:dim], devices, lengths[dim] // devices, *lengths[dim + 1 :])
    return jnp.moveaxis(blocks, dim, 0)


def sum_at_owner(value, axis, dim):
    devices = lax.axis_size(axis)
    blocks = lax.all_to_all(cut_along(value, dim, devices), axis, 0, 0, tiled=True)
    return jnp.sum(blocks.astype(jnp.float32), axis=0)


def sent_together_2(arrays, axis, dim, along):
    columns = [a.reshape(*a.shape[:along], -1) for a in arrays]
    both = jnp.concatenate(columns, axis=along)
    filled, at, gathered = (sum_at_owner(both, axis, dim), 0, [])
    for a, column in zip(arrays, columns):
        piece = filled[..., at : at + column.shape[along]]
        gathered.append(piece.reshape(*piece.shape[:along], *a.shape[along:]))
        at += column.shape[along]
    return tuple(gathered)


def rms_forward(values, gain):
    inverse = lax.rsqrt(jnp.mean(values * values, axis=-1, keepdims=True) + EPS)
    return (values * inverse * gain, inverse)


def rms_backward(values, inverse, gain, grad):
    normal = values * inverse
    grad_gain = jnp.sum(grad * normal, axis=0)
    scaled = grad * gain
    grad_in = inverse * (scaled - normal * jnp.mean(scaled * normal, axis=-1, keepdims=True))
    return (grad_in, grad_gain)


def rotary_tables(positions):
    half_dim = HEAD // 2
    inv_freq = 10000.0 ** (-jnp.arange(half_dim, dtype=jnp.float32) / half_dim)
    angles = positions.astype(jnp.float32)[:, None] * inv_freq[None, :]
    return (jnp.cos(angles)[:, None, :], jnp.sin(angles)[:, None, :])


def rotate(values, cosines, sines):
    first, second = jnp.split(values, 2, axis=-1)
    return jnp.concatenate(
        [first * cosines - second * sines, second * cosines + first * sines], axis=-1
    )


def rotate_back(grad, cosines, sines):
    grad_first, grad_second = jnp.split(grad, 2, axis=-1)
    return jnp.concatenate(
        [grad_first * cosines + grad_second * sines, grad_second * cosines - grad_first * sines],
        axis=-1,
    )


def contract_rows(left, right):
    return lax.dot_general(
        left, right, (((0,), (0,)), ((), ())), preferred_element_type=jnp.float32
    )


def contract_cols(left, right):
    return lax.dot_general(
        left, right, (((1,), (1,)), ((), ())), preferred_element_type=jnp.float32
    )


def key_blocks(piece_keys, piece_values, carry, step):
    rows = piece_keys.shape[0]
    width = KEY_BLOCK
    count = rows // width
    keys = piece_keys.reshape(count, width, KV_HEADS, HEAD)
    vals = piece_values.reshape(count, width, KV_HEADS, HEAD)
    starts = width * jnp.arange(count, dtype=jnp.int32)

    def one(state, inputs):
        state = step(state, inputs[0], inputs[1], inputs[2])
        return (state, None)

    carry, unused = lax.scan(one, carry, (keys, vals, starts))
    return carry


def masked_scores(q_heads, key_block, key_start, row_ids, scale):
    cols = key_start + jnp.arange(key_block.shape[0], dtype=jnp.int32)
    scores = (
        jnp.einsum("tkgd,pkd->kgtp", q_heads, key_block, preferred_element_type=jnp.float32) * scale
    )
    return jnp.where(cols[None, :] <= row_ids[:, None], scores, MASKED)


def attention_forward(queries, keys, values, row_ids, scale):
    rows = queries.shape[0]
    groups = HEADS // KV_HEADS
    q_heads = queries.reshape(rows, KV_HEADS, groups, HEAD)

    def step(state, key_block, value_block, key_start):
        top, total, accum = state
        scores = masked_scores(q_heads, key_block, key_start, row_ids, scale)
        new_top = jnp.maximum(top, jnp.max(scores, axis=-1))
        factor = jnp.exp(top - new_top)
        weights = jnp.exp(scores - new_top[..., None])
        total = total * factor + jnp.sum(weights, axis=-1)
        accum = accum * factor[..., None] + jnp.einsum(
            "kgtp,pkd->kgtd",
            weights.astype(jnp.bfloat16),
            value_block,
            preferred_element_type=jnp.float32,
        )
        return (new_top, total, accum)

    def fold(state, pieces, start):
        return key_blocks(pieces[0], pieces[1], state, step)

    init = (
        jnp.full((KV_HEADS, groups, rows), MASKED, jnp.float32),
        jnp.zeros((KV_HEADS, groups, rows), jnp.float32),
        jnp.zeros((KV_HEADS, groups, rows, HEAD), jnp.float32),
    )
    top, total, accum = fold(init, in_one_piece((keys, values), "ctx", 0, 1), jnp.int32(0))
    return (accum / total[..., None], top + jnp.log(total))


def attention_backward(queries, keys, values, row_ids, scale, outputs, log_total, grad_low):
    rows = queries.shape[0]
    groups = HEADS // KV_HEADS
    seq_rows = rows * lax.axis_size("ctx")
    q_heads = queries.reshape(rows, KV_HEADS, groups, HEAD)
    grad_heads = grad_low.reshape(rows, KV_HEADS, groups, HEAD)
    delta = jnp.einsum("tkgd,kgtd->kgt", grad_heads.astype(jnp.float32), outputs)

    def step(state, key_block, value_block, key_start):
        grad_q, grad_k, grad_v = state
        width = key_block.shape[0]
        scores = masked_scores(q_heads, key_block, key_start, row_ids, scale)
        probs = jnp.exp(scores - log_total[..., None])
        part_v = jnp.einsum(
            "kgtp,tkgd->pkd",
            probs.astype(jnp.bfloat16),
            grad_heads,
            preferred_element_type=jnp.float32,
        )
        grad_probs = jnp.einsum(
            "tkgd,pkd->kgtp", grad_heads, value_block, preferred_element_type=jnp.float32
        )
        grad_scores = (probs * (grad_probs - delta[..., None])).astype(jnp.bfloat16)
        grad_q = grad_q + jnp.einsum(
            "kgtp,pkd->kgtd", grad_scores, key_block, preferred_element_type=jnp.float32
        )
        part_k = (
            jnp.einsum("kgtp,tkgd->pkd", grad_scores, q_heads, preferred_element_type=jnp.float32)
            * scale
        )
        old_k = lax.dynamic_slice_in_dim(grad_k, key_start, width, 0)
        old_v = lax.dynamic_slice_in_dim(grad_v, key_start, width, 0)
        grad_k = lax.dynamic_update_slice_in_dim(grad_k, old_k + part_k, key_start, 0)
        grad_v = lax.dynamic_update_slice_in_dim(grad_v, old_v + part_v, key_start, 0)
        return (grad_q, grad_k, grad_v)

    def fold(state, pieces, start):
        return key_blocks(pieces[0], pieces[1], state, step)

    init = (
        jnp.zeros((KV_HEADS, groups, rows, HEAD), jnp.float32),
        jnp.zeros((seq_rows, KV_HEADS, HEAD), jnp.float32),
        jnp.zeros((seq_rows, KV_HEADS, HEAD), jnp.float32),
    )
    grad_q, grad_k, grad_v = fold(init, in_one_piece((keys, values), "ctx", 0, 1), jnp.int32(0))
    own_k, own_v = sent_together(
        (grad_k.reshape(seq_rows, KV_HEADS * HEAD), grad_v.reshape(seq_rows, KV_HEADS * HEAD)),
        "ctx",
        0,
        1,
    )
    grad_q = jnp.transpose(grad_q * scale, (2, 0, 1, 3))
    return (grad_q, own_k, own_v)


def body(
    layer_in,
    positions,
    norm_gain1,
    w_query,
    w_key,
    w_value,
    w_out,
    norm_gain2,
    w_gate,
    w_up,
    w_down,
    cotangent,
):
    rows = layer_in.shape[1]
    scale = HEAD ** (-0.5)
    row_ids = lax.axis_index("ctx") * rows + jnp.arange(rows, dtype=jnp.int32)
    gathered = (
        *in_one_piece_2(
            (norm_gain1, w_query, w_key, w_value, w_out, norm_gain2, w_gate, w_up), "dp", 0, 1
        ),
        lax.all_gather(w_down, "dp", axis=0, tiled=True),
    )
    gain1, wq, wk, wv, wo, gain2, wg, wu, wd = gathered
    gain1 = gain1.astype(jnp.float32)
    gain2 = gain2.astype(jnp.float32)
    cosines, sines = rotary_tables(positions[0])
    x = layer_in[0].astype(jnp.float32)
    h1f, inverse1 = rms_forward(x, gain1)
    h1 = h1f.astype(jnp.bfloat16)
    q_lin = jnp.dot(h1, wq, preferred_element_type=jnp.float32).reshape(rows, HEADS, HEAD)
    k_lin = jnp.dot(h1, wk, preferred_element_type=jnp.float32).reshape(rows, KV_HEADS, HEAD)
    values = jnp.dot(h1, wv, preferred_element_type=jnp.float32).astype(jnp.bfloat16)
    queries = rotate(q_lin, cosines, sines).astype(jnp.bfloat16).reshape(rows, HEADS * HEAD)
    keys = rotate(k_lin, cosines, sines).astype(jnp.bfloat16).reshape(rows, KV_HEADS * HEAD)
    outputs, log_total = attention_forward(queries, keys, values, row_ids, scale)
    attn = jnp.transpose(outputs, (2, 0, 1, 3)).reshape(rows, HEADS * HEAD).astype(jnp.bfloat16)
    x2 = x + jnp.dot(attn, wo, preferred_element_type=jnp.float32)
    h2f, inverse2 = rms_forward(x2, gain2)
    h2 = h2f.astype(jnp.bfloat16)
    gate = jnp.dot(h2, wg, preferred_element_type=jnp.float32)
    up = jnp.dot(h2, wu, preferred_element_type=jnp.float32)
    sigma = jax.nn.sigmoid(gate)
    active = gate * sigma
    hidden = (active * up).astype(jnp.bfloat16)
    result = x2 + jnp.dot(hidden, wd, preferred_element_type=jnp.float32)
    grad_y = cotangent[0].astype(jnp.float32)
    grad_y_low = grad_y.astype(jnp.bfloat16)
    grad_down = contract_rows(hidden, grad_y_low)
    grad_hidden = contract_cols(grad_y_low, wd)
    grad_act = grad_hidden * up
    grad_gate_low = (grad_act * (sigma + gate * sigma * (1.0 - sigma))).astype(jnp.bfloat16)
    grad_up_low = (grad_hidden * active).astype(jnp.bfloat16)
    grad_gate = contract_rows(h2, grad_gate_low)
    grad_up = contract_rows(h2, grad_up_low)
    grad_h2 = contract_cols(grad_gate_low, wg) + contract_cols(grad_up_low, wu)
    grad_norm2, grad_gain2 = rms_backward(x2, inverse2, gain2, grad_h2)
    grad_x2 = grad_y + grad_norm2
    grad_attn_low = grad_x2.astype(jnp.bfloat16)
    grad_out = contract_rows(attn, grad_attn_low)
    grad_o_low = contract_cols(grad_attn_low, wo).astype(jnp.bfloat16)
    grad_q, grad_k, grad_v = attention_backward(
        queries, keys, values, row_ids, scale, outputs, log_total, grad_o_low
    )
    grad_q_lin = (
        rotate_back(grad_q.reshape(rows, HEADS, HEAD), cosines, sines)
        .reshape(rows, HEADS * HEAD)
        .astype(jnp.bfloat16)
    )
    grad_k_lin = (
        rotate_back(grad_k.reshape(rows, KV_HEADS, HEAD), cosines, sines)
        .reshape(rows, KV_HEADS * HEAD)
        .astype(jnp.bfloat16)
    )
    grad_v_low = grad_v.astype(jnp.bfloat16)
    grad_query = contract_rows(h1, grad_q_lin)
    grad_key = contract_rows(h1, grad_k_lin)
    grad_value = contract_rows(h1, grad_v_low)
    grad_h1 = (
        contract_cols(grad_q_lin, wq)
        + contract_cols(grad_k_lin, wk)
        + contract_cols(grad_v_low, wv)
    )
    grad_norm1, grad_gain1 = rms_backward(x, inverse1, gain1, grad_h1)
    grad_x = grad_x2 + grad_norm1
    shares = (
        *sent_together_2(
            (
                grad_gain1.astype(jnp.bfloat16),
                grad_query.astype(jnp.bfloat16),
                grad_key.astype(jnp.bfloat16),
                grad_value.astype(jnp.bfloat16),
                grad_out.astype(jnp.bfloat16),
                grad_gain2.astype(jnp.bfloat16),
                grad_gate.astype(jnp.bfloat16),
                grad_up.astype(jnp.bfloat16),
            ),
            "dp",
            0,
            1,
        ),
        sum_at_owner(grad_down.astype(jnp.bfloat16), "dp", 0),
    )
    totals = lax.psum(
        (
            shares[0],
            shares[1],
            shares[2],
            shares[3],
            shares[4],
            shares[5],
            shares[6],
            shares[7],
            shares[8],
        ),
        "ctx",
    )
    return (
        result.astype(jnp.bfloat16)[None],
        grad_x.astype(jnp.bfloat16)[None],
        totals[0],
        totals[1],
        totals[2],
        totals[3],
        totals[4],
        totals[5],
        totals[6],
        totals[7],
        totals[8],
    )


def solution(mesh):
    return jax.shard_map(
        body,
        mesh=mesh,
        in_specs=(
            P("dp", "ctx", None),
            P("dp", "ctx"),
            P("dp"),
            P("dp", None),
            P("dp", None),
            P("dp", None),
            P("dp", None),
            P("dp"),
            P("dp", None),
            P("dp", None),
            P("dp", None),
            P("dp", "ctx", None),
        ),
        out_specs=(
            P("dp", "ctx", None),
            P("dp", "ctx", None),
            P("dp"),
            P("dp", None),
            P("dp", None),
            P("dp", None),
            P("dp", None),
            P("dp"),
            P("dp", None),
            P("dp", None),
            P("dp", None),
        ),
        check_vma=False,
    )
```

profile of v0, /device:TPU:0, one launch (start us, length us, event | category | flops | bytes accessed | tf_op | source)
XLA Modules:
  0.0 1054.1 jit_solution(2873456098684274314)
XLA Ops:
  8.8 6.1 concatenate.45
  16.0 19.7 %all-gather.4.cloned.1.call-done = bf16[576,4610]{1,0:T(8,128)(2,1)} async-done(((bf16[288,4610]{1,0:T(8,128)(2,1)}), bf16[576,4610]{1,0:T(8,128)(2,1)}) %all-gather.4.cloned.1.call-update) | async-done | bytes 5310736 | tf_op jit(solution)/shard_map/all_gather | solution.py:37
  44.2 86.0 %all-gather.6.cloned.1.call-done = bf16[8192,384]{0,1:T(8,128)(2,1)} async-done(((bf16[128,384]{0,1:T(8,128)(2,1)}), bf16[8192,384]{0,1:T(8,128)(2,1)}) %all-gather.6.cloned.1.call-update) | async-done | bytes 6291472 | tf_op jit(solution)/shard_map/all_gather | solution.py:18
  130.2 3.2 fusion.105
  134.8 3.4 copy.59
  139.5 3.4 copy.60
  142.9 81.1 %while.30 = (s32[]{:T(128)}, f32[3,3,128]{2,1,0:T(4,128)S(1)}, f32[3,3,128]{2,1,0:T(4,128)S(1)}, f32[3,3,128,64]{2,3,1,0:T(8,128)S(1)}, s32[16]{0:T(128)S(1)}, /...) while((s32[]{:T(128)}, f32[3,3,128]{2,1,0:T(4,128)S(1)}, ...), condition=%wide.region_4.5_spmd.clone, body=%wide.region_1.4_spmd.clone.sunk | while | flops 157776128 | bytes 8549533 | solution.py:127
  226.3 2.5 fusion.50
  228.8 2.4 fusion.54
  231.3 3.0 multiply_convert_fusion.1
  234.2 2.6 fusion.48
  236.9 3.1 multiply_reduce_fusion
  244.6 3.3 broadcast.154
  247.9 3.4 broadcast.154.clone
  251.3 327.7 %while.31 = (s32[]{:T(128)}, f32[3,3,128,64]{2,3,1,0:T(8,128)}, f32[8192,3,64]{0,2,1:T(8,128)}, f32[8192,3,64]{0,2,1:T(8,128)}, s32[16]{0:T(128)S(1)}, /*index=5...) while((s32[]{:T(128)}, f32[3,3,128,64]{2,3,1,0:T(8,128)}, ...), condition=%wide.region_8.9_spmd.clone, body=%wide.region_7.8_spmd.clone.sunk | while | flops 383894144 | bytes 17227188 | solution.py:127
  260.6 2.4 fusion.176
  263.0 3.5 dynamic_update_slice.10
  268.4 3.4 dynamic_update_slice.11
  281.2 2.4 fusion.176
  283.6 3.5 dynamic_update_slice.10
  289.0 3.4 dynamic_update_slice.11
  301.9 2.4 fusion.176
  304.2 3.5 dynamic_update_slice.10
  309.6 3.4 dynamic_update_slice.11
  322.5 2.4 fusion.176
  324.8 3.4 dynamic_update_slice.10
  330.2 3.4 dynamic_update_slice.11
  343.1 2.4 fusion.176
  345.4 3.4 dynamic_update_slice.10
  350.8 3.4 dynamic_update_slice.11
  363.7 2.4 fusion.176
  366.0 3.4 dynamic_update_slice.10
  371.4 3.3 dynamic_update_slice.11
  386.6 3.4 dynamic_update_slice.10
  391.9 3.3 dynamic_update_slice.11
  404.7 2.4 fusion.176
  407.1 3.4 dynamic_update_slice.10
  412.4 3.3 dynamic_update_slice.11
  427.6 3.5 dynamic_update_slice.10
  433.0 3.3 dynamic_update_slice.11
  448.2 3.4 dynamic_update_slice.10
  453.5 3.4 dynamic_update_slice.11
  466.4 2.4 fusion.176
  468.7 3.4 dynamic_update_slice.10
  474.1 3.3 dynamic_update_slice.11
  486.9 2.4 fusion.176
  489.2 3.4 dynamic_update_slice.10
  494.6 3.4 dynamic_update_slice.11
  509.8 3.4 dynamic_update_slice.10
  515.1 3.4 dynamic_update_slice.11
  530.4 3.4 dynamic_update_slice.10
  535.7 3.4 dynamic_update_slice.11
  550.9 3.4 dynamic_update_slice.10
  556.3 3.4 dynamic_update_slice.11
  571.4 2.9 dynamic_update_slice.10
  576.2 2.7 dynamic_update_slice.11
  579.0 10.5 pad_maximum_fusion
  593.1 3.8 all-to-all-start.1
  597.2 2.4 all-to-all-done.1
  607.5 212.0 %reduce-scatter.2.cloned.1.call-done = f32[128,384]{0,1:T(8,128)} async-done(((f32[8192,384]{0,1:T(8,128)}), f32[128,384]{0,1:T(8,128)}) %reduce-scatter.2.cloned.1.call-update) | async-done | bytes 196624 | tf_op jit(solution)/shard_map/reduce_scatter | solution.py:27
  828.3 10.3 concatenate.60
  838.6 9.6 all_to_all.10
  852.1 2.8 fusion.106
  859.0 176.8 %all-reduce = (f32[288]{0:T(512)}, f32[288]{0:T(512)}) all-reduce(f32[288]{0:T(512)S(1)} %get-tuple-element.269, f32[288]{0:T(512)S(1)} %get-tuple-element.268), channel_id=1, replica_groups=mesh['dp'=2,'ctx'=64] {'ctx'}, use_global_device_ids=true, to_apply=%region_14.15 | all-reduce | flops 576 | bytes 4608 | tf_op jit(solution)/shard_map/psum | solution.py:329
  (677 shorter events, 307.1 us)
Async XLA Ops:
  7.2 28.5 %all-gather.4.cloned.1.call-start = ((), (), s32[]{:S(2)}) async-start(), calls=%async_computation.3 | async-start | bytes 8183808 | tf_op jit(solution)/shard_map/all_gather | solution.py:37
  14.9 115.3 %all-gather.6.cloned.1.call-start = ((), (), s32[]{:S(2)}) async-start(), calls=%async_computation.4 | async-start | bytes 6389760 | tf_op jit(solution)/shard_map/all_gather | solution.py:18
  15.9 27.7 %copy-start.35 = (f32[128]{0:T(128)}, f32[128]{0:T(128)S(1)}, u32[]{:S(2)}) copy-start(f32[128]{0:T(128)S(1)} %add_rsqrt_fusion.1) | copy-start | bytes 1540
  16.0 28.0 %copy-start.25 = (f32[128,32]{0,1:T(8,128)}, f32[128,32]{0,1:T(8,128)S(1)}, u32[]{:S(2)}) copy-start(f32[128,32]{0,1:T(8,128)S(1)} %get-tuple-element.351) | copy-start | bytes 49156
  38.3 5.3 copy-start.32
  40.9 190.3 %all-gather.8.cloned.1.call-start = ((), (), s32[]{:S(2)}) async-start(), calls=%async_computation.5 | async-start | bytes 2654208 | tf_op jit(solution)/shard_map/all_gather | solution.py:247
  41.6 777.8 %reduce-scatter.2.cloned.1.call-start = ((), (), s32[]{:S(2)}) async-start(), calls=%async_computation.6 | async-start | bytes 12779520 | tf_op jit(solution)/shard_map/reduce_scatter | solution.py:27
  226.1 14.4 %copy-start.8 = (f32[128,576]{0,1:T(8,128)}, f32[128,576]{0,1:T(8,128)S(1)}, u32[]{:S(2)}) copy-start(f32[128,576]{0,1:T(8,128)S(1)} %get-tuple-element.353) | copy-start | bytes 884740
  226.3 4.9 copy-start.21
  234.2 5.7 copy-start.27
  234.2 5.7 copy-start.29
  240.7 7.2 copy-start.10
  266.5 5.3 copy-start.1
  266.5 5.3 copy-start.43
  287.1 5.3 copy-start.1
  287.1 5.3 copy-start.43
  307.7 5.3 copy-start.1
  307.7 5.3 copy-start.43
  328.3 5.3 copy-start.1
  328.3 5.3 copy-start.43
  348.9 5.3 copy-start.1
  348.9 5.3 copy-start.43
  369.5 5.2 copy-start.1
  369.5 5.2 copy-start.43
  390.0 5.2 copy-start.1
  390.0 5.2 copy-start.43
  410.5 5.2 copy-start.1
  410.5 5.2 copy-start.43
  431.1 5.3 copy-start.1
  431.1 5.3 copy-start.43
  451.6 5.3 copy-start.1
  451.6 5.3 copy-start.43
  472.2 5.2 copy-start.1
  472.2 5.2 copy-start.43
  477.4 3.6 copy-start.38
  492.7 5.3 copy-start.1
  492.7 5.3 copy-start.43
  513.2 5.3 copy-start.1
  513.2 5.3 copy-start.43
  533.8 5.3 copy-start.1
  533.8 5.3 copy-start.43
  554.4 5.3 copy-start.1
  554.4 5.3 copy-start.43
  574.3 4.6 copy-start.1
  574.3 4.6 copy-start.43
  593.1 3.9 copy-start.3
  593.1 4.0 copy-start.26
  593.1 6.5 all-to-all-start.1
  597.0 439.7 %all-reduce.4.cloned.1.call-start = ((), (), s32[]{:S(2)}) async-start(), calls=%async_computation.7 | async-start | bytes 14745600 | tf_op jit(solution)/shard_map/psum | solution.py:329
  597.0 4.0 copy-start.5
  597.0 4.0 copy-start.33
  597.0 4.0 copy-start.36
  597.2 4.3 copy-start.11
  597.2 4.3 copy-start.24
  601.1 4.0 copy-start.7
  601.1 4.0 copy-start.30
  601.5 4.1 copy-start.28
  605.0 215.7 %copy-start.31 = (f32[128,576]{0,1:T(8,128)S(1)}, f32[128,576]{0,1:T(8,128)}, u32[]{:S(2)}) copy-start(f32[128,576]{0,1:T(8,128)} %fusion.63) | copy-start | bytes 884740
  849.1 5.7 copy-start.2
  856.5 179.4 %copy-start.19 = (f32[128,576]{0,1:T(8,128)S(1)}, f32[128,576]{0,1:T(8,128)}, u32[]{:S(2)}) copy-start(f32[128,576]{0,1:T(8,128)} %get-tuple-element.355) | copy-start | bytes 884740
  856.5 179.4 %copy-start.34 = (f32[576]{0:T(1024)S(1)}, f32[576]{0:T(1024)}, u32[]{:S(2)}) copy-start(f32[576]{0:T(1024)} %copy-done.32) | copy-start | bytes 6916
  856.5 179.4 %copy-start.37 = (f32[128]{0:T(128)S(1)}, f32[128]{0:T(128)}, u32[]{:S(2)}) copy-start(f32[128]{0:T(128)} %copy-done.35) | copy-start | bytes 1540
  1036.6 5.6 copy-start.20
  1036.6 6.4 copy-start.15
  (91 other events, 233.8 us)
Sparse Core Ops, SparseCore 0:
  15.0 20.6 all-gather.3
  41.0 89.0 all-gather.5
  131.8 12.0 all-gather.7
  589.7 229.7 reduce-scatter.1
  855.0 153.6 all-reduce.3
where the time goes:
time: 1060 us; the launch traced here: 1050 us
  waiting for transfers between devices  321 us (30%)
  matrix products  239 us (23%)
  local copies, waits for them, and re-layouts  204 us (19%)
  blocking collectives  186 us (18%)
  other arithmetic  52.2 us (5%)
  loops' own time  33.5 us (3%)
  between operations  14.4 us (1%)
    reduce_scatter x1, waiting for transfers between devices, sent_together(): lax.psum_scatter(both, axis, scatter_dimension=dim, tiled=True)  212 us
    psum x1, blocking collectives, body(): lax.psum((shares[0], shares[1], shares[2], shares[3], shares[4], shares[5...  177 us
    all_gather x1, waiting for transfers between devices, in_one_piece(): lax.all_gather(both, axis, axis=dim, tiled=True)  86 us
    dynamic_update_slice x16, local copies, waits for them, and re-layouts, step(): lax.dynamic_update_slice_in_dim(grad_k, old_k + part_k, key_start, 0)  54.5 us
    dynamic_update_slice x16, local copies, waits for them, and re-layouts, step(): lax.dynamic_update_slice_in_dim(grad_v, old_v + part_v, key_start, 0)  53.2 us
    dot_general x32, matrix products, masked_scores(): jnp.einsum('tkgd,pkd->kgtp', q_heads, key_block, preferred_element_type=j...  47.7 us
    dot_general x16, matrix products, step(): jnp.einsum('kgtp,tkgd->pkd', grad_scores, q_heads, preferred_element_type...  37.6 us
    dot_general x16, matrix products, step(): jnp.einsum('kgtp,pkd->kgtd', grad_scores, key_block, preferred_element_ty...  33.6 us
  transfers between devices with their start and end apart: 6, of which 4 were waited for; matrix products, arithmetic and copies ran while one was open for 11% of the time, Pallas kernels for 0%

commit v1 on v0

v1 whole, which is shorter than its diff:
```python
import jax
import jax.numpy as jnp
from jax import lax
from jax.experimental import pallas as pl
from jax.experimental.pallas import tpu as pltpu
from jax.sharding import PartitionSpec as P

HEADS = 9
KV_HEADS = 3
GROUPS = HEADS // KV_HEADS
HEAD = 64
D = 576
FF = 1536
EPS = 1e-05
MASKED = -1e30
HALF = 64
GROUP = 8
KEYS = GROUP * HALF
ROWS = 2 * HALF
MESH = pl.DeviceIdType.MESH
F32 = jnp.float32
BF16 = jnp.bfloat16
VMEM_LIMIT = 60 * 1024 * 1024

E_GATE = 0
E_UP = 12 * 288
E_DOWN = 24 * 288
E_OUT = E_DOWN + 5 * 768
E_GAIN = E_OUT + 5 * 288
E_ROWS = 3 * 64 * 64


def vmem(n):
    return [pl.BlockSpec(memory_space=pltpu.VMEM)] * n


def anywhere(n):
    return [pl.BlockSpec(memory_space=pl.ANY)] * n


def shape(dims, dtype):
    return jax.ShapeDtypeStruct(dims, dtype)


def nn(a, b):
    return jnp.dot(a, b, preferred_element_type=F32)


def nt(a, b):
    return lax.dot_general(a, b, (((1,), (1,)), ((), ())), preferred_element_type=F32)


def tn(a, b):
    return lax.dot_general(a, b, (((0,), (0,)), ((), ())), preferred_element_type=F32)


def run_together(*tasks):
    tasks = list(tasks)
    while tasks:
        for task in list(tasks):
            try:
                next(task)
            except StopIteration:
                tasks.remove(task)


class Place:
    def __init__(self):
        self.core = lax.axis_index("dp")
        self.me = lax.axis_index("ctx")
        self.at = [lax.rem(self.me // 4**a, 4) for a in range(3)]

    def toward(self, axis, step):
        there = lax.rem(self.at[axis] + step, 4)
        return self.me + (there - self.at[axis]) * 4**axis

    def coord(self, axis, step):
        return lax.rem(self.at[axis] + step, 4)

    def region(self, part, phase, coord):
        index = [None, None, None]
        for k in range(3):
            axis = (part + k) % 3
            index[2 - axis] = pl.ds(0, 4) if k < phase else coord if k == phase else self.at[axis]
        return tuple(index)


def send(src, dst, send_sem, recv_sem, device):
    copy = pltpu.make_async_remote_copy(
        src_ref=src, dst_ref=dst, send_sem=send_sem, recv_sem=recv_sem, device_id=device, device_id_type=MESH
    )
    copy.start()
    return copy


def arrived(dst, send_sem, recv_sem, device):
    pltpu.make_async_remote_copy(
        src_ref=dst, dst_ref=dst, send_sem=send_sem, recv_sem=recv_sem, device_id=device, device_id_type=MESH
    ).wait_recv()


def gather_task(place, buf, rows, ssem, rsem, done):
    first, second, whole = pl.ds(0, rows // 2), pl.ds(rows // 2, rows // 2), None
    sent = []
    for phase in range(3):
        for part in range(3):
            axis = (part + phase) % 3
            plus, minus = {"ctx": place.toward(axis, 1)}, {"ctx": place.toward(axis, 3)}
            own = place.region(part, phase, place.at[axis])
            for k, (half, to) in enumerate(((first, plus), (second, minus), (second, plus), (first, minus))):
                ref = buf.at[(part, *own, half)]
                sent.append(send(ref, ref, ssem.at[part, phase, k], rsem.at[part, phase, k], to))
        yield
        for part in range(3):
            axis = (part + phase) % 3
            plus, minus = {"ctx": place.toward(axis, 1)}, {"ctx": place.toward(axis, 3)}
            for k, (half, step, to) in enumerate(((first, 3, plus), (second, 1, minus))):
                ref = buf.at[(part, *place.region(part, phase, place.coord(axis, step)), half)]
                arrived(ref, ssem.at[part, phase, k], rsem.at[part, phase, k], to)
                sent.append(send(ref, ref, ssem.at[part, phase, 4 + k], rsem.at[part, phase, 4 + k], to))
        yield
        for part in range(3):
            axis = (part + phase) % 3
            plus = {"ctx": place.toward(axis, 1)}
            for k, half, step in ((2, second, 3), (3, first, 1), (4, first, 2), (5, second, 2)):
                ref = buf.at[(part, *place.region(part, phase, place.coord(axis, step)), half)]
                arrived(ref, ssem.at[part, phase, k], rsem.at[part, phase, k], plus)
        done(phase)
    yield
    for copy in sent:
        copy.wait_send()


def add_into(buf, index, other):
    buf[index] = (buf[index].astype(F32) + other.astype(F32)).astype(BF16)


def scatter_task(place, buf, halves, wholes, rows, ssem, rsem, finish):
    first, second = pl.ds(0, rows // 2), pl.ds(rows // 2, rows // 2)
    sent = []
    for turn in range(3):
        phase = 2 - turn
        half_buf, whole_buf = halves[turn], wholes[turn]
        for part in range(3):
            axis = (part + phase) % 3
            plus, minus = {"ctx": place.toward(axis, 1)}, {"ctx": place.toward(axis, 3)}
            far = place.region(part, phase, place.coord(axis, 2))
            right = place.region(part, phase, place.coord(axis, 1))
            left = place.region(part, phase, place.coord(axis, 3))
            lead = (slice(None),) * phase
            for k, src, dst, to in (
                (0, (*far, first), half_buf.at[part, 0], plus),
                (1, (*far, second), half_buf.at[part, 1], minus),
                (2, (*right, second), whole_buf.at[(part, 0, *lead, second)], plus),
                (3, (*left, first), whole_buf.at[(part, 1, *lead, first)], minus),
            ):
                sent.append(send(buf.at[(part, *src)], dst, ssem.at[part, turn, k], rsem.at[part, turn, k], to))
        yield
        for part in range(3):
            axis = (part + phase) % 3
            plus, minus = {"ctx": place.toward(axis, 1)}, {"ctx": place.toward(axis, 3)}
            lead = (slice(None),) * phase
            for k, half, step, to in ((0, first, 1, plus), (1, second, 3, minus)):
                arrived(half_buf.at[part, k], ssem.at[part, turn, k], rsem.at[part, turn, k], to)
                index = (part, *place.region(part, phase, place.coord(axis, step)), half)
                add_into(buf, index, half_buf[part, k])
                dst = whole_buf.at[(part, k, *lead, half)]
                sent.append(send(buf.at[index], dst, ssem.at[part, turn, 4 + k], rsem.at[part, turn, 4 + k], to))
        yield
        for part in range(3):
            axis = (part + phase) % 3
            plus = {"ctx": place.toward(axis, 1)}
            lead = (slice(None),) * phase
            for k, side, half in ((2, 0, second), (3, 1, first), (4, 0, first), (5, 1, second)):
                dst = whole_buf.at[(part, side, *lead, half)]
                arrived(dst, ssem.at[part, turn, k], rsem.at[part, turn, k], plus)
            index = (part, *place.region(part, phase, place.at[axis]))
            total = buf[index].astype(F32) + whole_buf[part, 0].astype(F32) + whole_buf[part, 1].astype(F32)
            if turn < 2:
                buf[index] = total.astype(BF16)
            else:
                finish(part, index, total)
    yield
    for copy in sent:
        copy.wait_send()


def small_sum_task(place, buf, slots, out, ssem, rsem, ssem2, rsem2):
    sent = []
    for turn in range(3):
        phase = 2 - turn
        for part in range(3):
            axis = (part + phase) % 3
            for k in range(3):
                src = buf.at[(part, *place.region(part, phase, place.coord(axis, k + 1)))]
                to = {"ctx": place.toward(axis, k + 1)}
                sent.append(send(src, slots[turn].at[part, k], ssem.at[part, turn, k], rsem.at[part, turn, k], to))
        yield
        for part in range(3):
            axis = (part + phase) % 3
            index = (part, *place.region(part, phase, place.at[axis]))
            total = buf[index].astype(F32)
            for k in range(3):
                to = {"ctx": place.toward(axis, k + 1)}
                arrived(slots[turn].at[part, k], ssem.at[part, turn, k], rsem.at[part, turn, k], to)
                total = total + slots[turn][part, k].astype(F32)
            if turn < 2:
                buf[index] = total.astype(BF16)
            else:
                out[index] = total.astype(BF16)
    for phase in range(3):
        for part in range(3):
            axis = (part + phase) % 3
            ref = out.at[(part, *place.region(part, phase, place.at[axis]))]
            for k in range(3):
                to = {"ctx": place.toward(axis, k + 1)}
                sent.append(send(ref, ref, ssem2.at[part, phase, k], rsem2.at[part, phase, k], to))
        yield
        for part in range(3):
            axis = (part + phase) % 3
            for k in range(3):
                to = {"ctx": place.toward(axis, k + 1)}
                ref = out.at[(part, *place.region(part, phase, place.coord(axis, 3 - k)))]
                arrived(ref, ssem2.at[part, phase, k], rsem2.at[part, phase, k], to)
    yield
    for copy in sent:
        copy.wait_send()


def greet(place, steps, callers, targets):
    barrier = pltpu.get_barrier_semaphore()
    for axis in range(3):
        for step in steps:
            pl.semaphore_signal(barrier, inc=1, device_id={"ctx": place.toward(axis, step)}, device_id_type=MESH)
    pl.semaphore_signal(barrier, inc=1, device_id={"dp": 1 - place.core}, device_id_type=MESH)
    for caller in callers:

        @pl.when(caller != place.me)
        def _():
            pl.semaphore_signal(barrier, inc=1, device_id={"ctx": caller}, device_id_type=MESH)

    count = 3 * len(steps) + 1
    for target in targets:
        count = count + jnp.where(target != place.me, 1, 0)
    pl.semaphore_wait(barrier, count)


def folded(half_block):
    return jnp.where(half_block < 64, half_block, 127 - half_block)


def swap_halves(v):
    return jnp.concatenate([v[:, HEAD // 2 :], v[:, : HEAD // 2]], axis=1)


def rms_forward(values, gain):
    inverse = lax.rsqrt(jnp.mean(values * values, axis=-1, keepdims=True) + EPS)
    return values * inverse * gain, inverse


def rms_backward(values, inverse, gain, grad):
    normal = values * inverse
    grad_gain = jnp.sum(grad * normal, axis=0, keepdims=True)
    scaled = grad * gain
    grad_in = inverse * (scaled - normal * jnp.mean(scaled * normal, axis=-1, keepdims=True))
    return grad_in, grad_gain


def start_kernel(
    x_in, trig_in, cot_in, gains_in, wq_in, wk_in, wv_in, wo_in, wg_in, wu_in, wd_in,
    xz, trig, cotz, gains, wq, wk, wv, wo, wg, wu, wd, h1_out, qpad, kv,
    zig_send, zig_recv, zig_local, dp_send, dp_recv, dp_local, ssem, rsem,
):
    place = Place()
    me = place.me
    targets = [folded(2 * me + k) for k in range(2)]
    owners = [me // 2, (127 - me) // 2]
    greet(place, (1, 3), owners, targets)
    slot = me // 32
    moved = ((x_in, xz), (trig_in, trig), (cot_in, cotz))

    def zig(k, n, src, dst):
        return src.at[pl.ds(HALF * k, HALF)], dst.at[pl.ds(pl.multiple_of(slot * HALF, HALF), HALF)]

    for n, (src, dst) in enumerate(moved):
        for k in range(2):
            a, b = zig(k, n, src, dst)

            @pl.when(targets[k] != me)
            def _():
                send(a, b, zig_send.at[n, k], zig_recv.at[n, slot], {"ctx": targets[k]})

            @pl.when(targets[k] == me)
            def _():
                pltpu.make_async_copy(a, b, zig_local.at[n]).start()

    other = {"dp": 1 - place.core}
    weights = ((gains_in, gains), (wq_in, wq), (wk_in, wk), (wv_in, wv), (wo_in, wo), (wg_in, wg), (wu_in, wu), (wd_in, wd))
    copies = []
    for n, (src, dst) in enumerate(weights):
        there = send(src, dst.at[place.core], dp_send.at[n], dp_recv.at[n], other)
        here = pltpu.make_async_copy(src, dst.at[place.core], dp_local.at[n])
        here.start()
        copies.append((there, here))

    def zig_wait(n):
        src, dst = moved[n]
        for side in range(2):
            ref = dst.at[pl.ds(side * HALF, HALF)]

            @pl.when(owners[side] != me)
            def _():
                arrived(ref, zig_send.at[n, 0], zig_recv.at[n, side], {"ctx": owners[side]})

            @pl.when(owners[side] == me)
            def _():
                pltpu.make_async_copy(ref, ref, zig_local.at[n]).wait()

    def dp_wait(n):
        dst = weights[n][1]
        copies[n][1].wait()
        arrived(dst.at[1 - place.core], dp_send.at[n], dp_recv.at[n], other)

    zig_wait(0)
    zig_wait(1)
    dp_wait(0)
    gain1 = jnp.concatenate([gains[0, 0:1, 0:288], gains[1, 0:1, 0:288]], axis=1)
    h1f, _ = rms_forward(xz[...].astype(F32), gain1)
    h1 = h1f.astype(BF16)
    h1_out[...] = h1
    for n in (1, 2, 3):
        dp_wait(n)

    def linear(w):
        return nn(h1[:, :288], w[0]) + nn(h1[:, 288:], w[1])

    cosines, sines = trig[:, 0:HEAD], trig[:, HEAD : 2 * HEAD]
    k_lin = linear(wk)
    v_lin = linear(wv)
    for h in range(KV_HEADS):
        cols = slice(h * HEAD, (h + 1) * HEAD)
        key = k_lin[:, cols]
        key = key * cosines + swap_halves(key) * sines
        kv[h, me // 16, lax.rem(me // 4, 4), lax.rem(me, 4)] = jnp.concatenate([key, v_lin[:, cols]], axis=1).astype(BF16)
    task = gather_task(place, kv, ROWS, ssem, rsem, lambda phase: None)
    next(task)
    q_lin = linear(wq)
    for h in range(HEADS):
        query = q_lin[:, h * HEAD : (h + 1) * HEAD]
        query = (query * cosines + swap_halves(query) * sines).astype(BF16)
        query = (query.astype(F32) * HEAD**-0.5).astype(BF16)
        query = jnp.concatenate([query, jnp.zeros((ROWS, HEAD), BF16)], axis=1)
        group = (h % GROUPS) * HALF
        qpad[h // GROUPS, group : group + HALF] = query[:HALF]
        qpad[h // GROUPS, 192 + group : 192 + group + HALF] = query[HALF:]
    run_together(task)
    zig_wait(2)
    for n in (4, 5, 6, 7):
        dp_wait(n)
    for there, _ in copies:
        there.wait_send()
    for n, (src, dst) in enumerate(moved):
        for k in range(2):

            @pl.when(targets[k] != me)
            def _():
                a, b = zig(k, n, src, dst)
                pltpu.make_async_remote_copy(
                    src_ref=a, dst_ref=b, send_sem=zig_send.at[n, k], recv_sem=zig_recv.at[n, slot],
                    device_id={"ctx": targets[k]}, device_id_type=MESH,
                ).wait_send()


def start_call(x, trig, cot, gains, weights):
    full = [shape((2, *w.shape), BF16) for w in weights]
    return pl.pallas_call(
        start_kernel,
        out_shape=(
            shape((ROWS, D), BF16), shape((ROWS, 128), F32), shape((ROWS, D), BF16), shape((2, 8, 384), F32),
            *full,
            shape((ROWS, D), BF16), shape((KV_HEADS, 384, 128), BF16), shape((KV_HEADS, 4, 4, 4, ROWS, 128), BF16),
        ),
        in_specs=anywhere(11),
        out_specs=(*vmem(7), *anywhere(4), *vmem(3)),
        scratch_shapes=[
            pltpu.SemaphoreType.DMA((3, 2)), pltpu.SemaphoreType.DMA((3, 2)), pltpu.SemaphoreType.DMA((3,)),
            pltpu.SemaphoreType.DMA((8,)), pltpu.SemaphoreType.DMA((8,)), pltpu.SemaphoreType.DMA((8,)),
            pltpu.SemaphoreType.DMA((3, 3, 6)), pltpu.SemaphoreType.DMA((3, 3, 6)),
        ],
        compiler_params=pltpu.CompilerParams(collective_id=0, has_side_effects=True, vmem_limit_bytes=VMEM_LIMIT),
        name="qkv_gather",
    )(x, trig, cot, gains, *weights)


def middle_kernel(
    xz, cotz, gains, qpad, kv, wo, wg, wu, wd, trig,
    result, e_out, dkv, dq_out, dx2_out,
    outs_t, lse, dopad, attn, dq_lin,
):
    me = lax.axis_index("ctx")
    mine = me // GROUP
    within = lax.rem(me, GROUP)
    key_row = lax.broadcasted_iota(jnp.int32, (KEYS, 384), 0)
    lane = lax.broadcasted_iota(jnp.int32, (KEYS, 384), 1)
    low_mask = key_row <= jnp.where(lane < 192, HALF * within + lax.rem(lane, HALF), KEYS)
    key_row = key_row[:, :192]
    lane = lane[:, :192]
    high_mask = lax.rem(key_row, HALF) - HALF * (key_row // HALF) <= lax.rem(lane, HALF) - HALF * within
    ones_lane = lax.broadcasted_iota(jnp.int32, (KEYS, 128), 1) < HEAD

    def keys_of(h, g, side):
        return kv[h, pl.ds(g * GROUP, GROUP), side * HALF : (side + 1) * HALF, :].reshape(KEYS, 128)

    def forward(h, _):
        def step(block, queries, mask, state):
            top, accum = state
            scores = nt(block, queries)
            if mask is not None:
                scores = jnp.where(mask, scores, MASKED)
            new_top = jnp.maximum(top, jnp.max(scores, axis=0, keepdims=True))
            weights = jnp.exp(scores - new_top).astype(BF16)
            values = jnp.where(ones_lane, jnp.ones_like(block), block)
            return new_top, accum * jnp.exp(top - new_top) + tn(values, weights)

        state = (jnp.full((1, 384), MASKED, F32), jnp.zeros((128, 384), F32))
        state = lax.fori_loop(0, mine, lambda g, s: step(keys_of(h, g, 0), qpad[h], None, s), state)
        top, accum = step(keys_of(h, mine, 0), qpad[h], low_mask, state)
        queries = qpad[h, 192:384]
        late = step(keys_of(h, mine, 1), queries, high_mask, (top[:, 192:], accum[:, 192:]))

        def both(g, s):
            s = step(keys_of(h, g, 0), queries, None, s)
            return step(keys_of(h, g, 1), queries, None, s)

        late = lax.fori_loop(mine + 1, 8, both, late)
        top = jnp.concatenate([top[:, :192], late[0]], axis=1)
        accum = jnp.concatenate([accum[:, :192], late[1]], axis=1)
        total = accum[0:1, :]
        outs = accum / total
        outs_t[h] = outs
        lse[h] = top + jnp.log(total)
        attn[h] = outs.T.astype(BF16)
        return 0

    lax.fori_loop(0, KV_HEADS, forward, 0)

    def by_token(ref, lanes):
        pieces = []
        for h in range(HEADS):
            group = (h % GROUPS) * HALF
            here = ref[h // GROUPS]
            pieces.append(jnp.concatenate([here[group : group + HALF, lanes], here[192 + group : 192 + group + HALF, lanes]], axis=0))
        return jnp.concatenate(pieces, axis=1)

    gain2 = jnp.concatenate([gains[0, 1:2, 0:288], gains[1, 1:2, 0:288]], axis=1)
    attn_low = by_token(attn, slice(64, 128))
    x = xz[...].astype(F32)
    x2 = x + nn(attn_low, wo[...])
    h2f, inverse2 = rms_forward(x2, gain2)
    h2 = h2f.astype(BF16)
    pad = jnp.zeros((ROWS, 64), BF16)
    dy_low = cotz[...]
    dy_pad = jnp.concatenate([dy_low, pad], axis=1)
    total = x2
    grad_h2 = jnp.zeros((ROWS, D), F32)

    def put(base, length, value, half, row):
        for tile in range(value.shape[1] // 128):
            at = base + tile * length + row
            e_out[half, at : at + value.shape[0], :] = value[:, tile * 128 : (tile + 1) * 128].astype(BF16)

    for t in range(3):
        cols = slice(512 * t, 512 * (t + 1))
        gate = nn(h2, wg[:, cols])
        up = nn(h2, wu[:, cols])
        sigma = jax.nn.sigmoid(gate)
        active = gate * sigma
        hidden = (active * up).astype(BF16)
        total = total + nn(hidden, wd[cols, :])
        grad_hidden = nt(dy_low, wd[cols, :])
        grad_gate = (grad_hidden * up * (sigma + active * (1.0 - sigma))).astype(BF16)
        grad_up = (grad_hidden * active).astype(BF16)
        grad_h2 = grad_h2 + nt(grad_gate, wg[:, cols]) + nt(grad_up, wu[:, cols])
        for base, value in ((E_GATE, tn(h2, grad_gate)), (E_UP, tn(h2, grad_up))):
            for half in range(2):
                put(base + 4 * t * 288, 288, value[288 * half : 288 * (half + 1)], half, 0)
        grad_down = tn(hidden, dy_pad)
        for s in range(2):
            index = 2 * t + s
            put(E_DOWN, 768, grad_down[256 * s : 256 * (s + 1)], index // 3, (index % 3) * 256)
    result[...] = total.astype(BF16)
    grad_norm2, grad_gain2 = rms_backward(x2, inverse2, gain2, grad_h2)
    grad_x2 = dy_low.astype(F32) + grad_norm2
    dx2_out[...] = grad_x2
    grad_attn = grad_x2.astype(BF16)
    grad_out = tn(attn_low, jnp.concatenate([grad_attn, pad], axis=1))
    for half in range(2):
        put(E_OUT, 288, grad_out[288 * half : 288 * (half + 1)], half, 0)
        line = jnp.concatenate([grad_gain2[:, 288 * half : 288 * (half + 1)], jnp.zeros((1, 96), F32)], axis=1)
        line = jnp.concatenate([line[:, 128 * k : 128 * (k + 1)] for k in range(3)] + [jnp.zeros((13, 128), F32)], axis=0)
        e_out[half, E_GAIN : E_GAIN + 16, :] = line.astype(BF16)
        e_out[half, E_GAIN + 16 : E_ROWS, :] = jnp.zeros((E_ROWS - E_GAIN - 16, 128), BF16)

    grad_o = nt(grad_attn, wo[...]).astype(BF16)
    for h in range(HEADS):
        piece = grad_o[:, h * HEAD : (h + 1) * HEAD]
        piece = jnp.concatenate([jnp.zeros((ROWS, HEAD), BF16), piece], axis=1)
        group = (h % GROUPS) * HALF
        dopad[h // GROUPS, group : group + HALF] = piece[:HALF]
        dopad[h // GROUPS, 192 + group : 192 + group + HALF] = piece[HALF:]

    def backward(h, _):
        delta = jnp.sum(dopad[h].astype(F32).T * outs_t[h], axis=0, keepdims=True)
        log_total = lse[h]

        def step(block, queries, grads, log_total, delta, mask, grad_q):
            scores = nt(block, queries)
            if mask is not None:
                scores = jnp.where(mask, scores, MASKED)
            probs = jnp.exp(scores - log_total)
            grad_scores = (probs * (nt(block, grads) - delta)).astype(BF16)
            part = nn(grad_scores, queries) + nn(probs.astype(BF16), grads)
            return grad_q + tn(block, grad_scores), part.astype(BF16)

        def save(g, side, part):
            dkv[h, pl.ds(g * GROUP, GROUP), side * HALF : (side + 1) * HALF, :] = part.reshape(GROUP, HALF, 128)

        def early(g, grad_q):
            grad_q, part = step(keys_of(h, g, 0), qpad[h], dopad[h], log_total, delta, None, grad_q)
            save(g, 0, part)
            save(g, 1, jnp.zeros((KEYS, 128), BF16))
            return grad_q

        grad_q = lax.fori_loop(0, mine, early, jnp.zeros((128, 384), F32))
        grad_q, part = step(keys_of(h, mine, 0), qpad[h], dopad[h], log_total, delta, low_mask, grad_q)
        save(mine, 0, part)
        queries, grads = qpad[h, 192:384], dopad[h, 192:384]
        log_late, delta_late = log_total[:, 192:], delta[:, 192:]
        late, part = step(keys_of(h, mine, 1), queries, grads, log_late, delta_late, high_mask, grad_q[:, 192:])
        save(mine, 1, part)

        def both(g, late):
            for side in range(2):
                late, part = step(keys_of(h, g, side), queries, grads, log_late, delta_late, None, late)
                save(g, side, part)
            return late

        late = lax.fori_loop(mine + 1, 8, both, late)
        dq_lin[h] = jnp.concatenate([grad_q[:, :192], late], axis=1).T
        return 0

    lax.fori_loop(0, KV_HEADS, backward, 0)
    cosines, sines = trig[:, 0:HEAD], trig[:, HEAD : 2 * HEAD]
    grad_q = by_token(dq_lin, slice(0, 64)) * HEAD**-0.5
    pieces = []
    for h in range(HEADS):
        piece = grad_q[:, h * HEAD : (h + 1) * HEAD]
        pieces.append(piece * cosines - swap_halves(piece) * sines)
    dq_out[...] = jnp.concatenate(pieces, axis=1).astype(BF16)


def middle_call(xz, cotz, gains, qpad, kv, wo, wg, wu, wd, trig):
    return pl.pallas_call(
        middle_kernel,
        out_shape=(
            shape((ROWS, D), BF16), shape((2, E_ROWS, 128), BF16), shape((KV_HEADS, 64, ROWS, 128), BF16),
            shape((ROWS, D), BF16), shape((ROWS, D), F32),
        ),
        in_specs=vmem(10),
        out_specs=tuple(vmem(5)),
        scratch_shapes=[
            pltpu.VMEM((KV_HEADS, 128, 384), F32), pltpu.VMEM((KV_HEADS, 1, 384), F32),
            pltpu.VMEM((KV_HEADS, 384, 128), BF16), pltpu.VMEM((KV_HEADS, 384, 128), BF16),
            pltpu.VMEM((KV_HEADS, 384, 128), F32),
        ],
        compiler_params=pltpu.CompilerParams(vmem_limit_bytes=VMEM_LIMIT),
        name="attention_and_ffn",
    )(xz, cotz, gains, qpad, kv, wo, wg, wu, wd, trig)


def end_kernel(
    dkv_in, e_in, dq, dx2, xz, h1, trig, gains, wq, wk, wv, result,
    e_sum, l_sum, out_result, out_grad,
    dkv, e_work, e_peer, l_full, l_peer, l_work, own, grad_z,
    kh0, kh1, kh2, kw0, kw1, kw2, eh0, eh1, eh2, ew0, ew1, ew2, ls0, ls1, ls2,
    ks, kr, es, er, gs, gr, ls, lr, ls2s, ls2r, dps, dpr, zs, zr, zl, local,
):
    place = Place()
    me, core = place.me, place.core
    owners = [me // 2, (127 - me) // 2]
    sources = [folded(2 * me + k) for k in range(2)]
    load = pltpu.make_async_copy(dkv_in, dkv, local.at[0])
    load.start()
    greet(place, (1, 2, 3), sources, owners)
    other = {"dp": 1 - core}
    e_copy = send(e_in.at[1 - core], e_peer, dps.at[0], dpr.at[0], other)
    e_load = pltpu.make_async_copy(e_in.at[core], e_work, local.at[1])
    e_load.start()

    def zig_send(n, src, dst):
        for side in range(2):
            half = (me, 127 - me)[side]
            k = lax.rem(half, 2)
            a = src.at[pl.ds(side * HALF, HALF)]
            b = dst.at[pl.ds(pl.multiple_of(k * HALF, HALF), HALF)]

            @pl.when(owners[side] != me)
            def _():
                send(a, b, zs.at[n, side], zr.at[n, k], {"ctx": owners[side]})

            @pl.when(owners[side] == me)
            def _():
                pltpu.make_async_copy(a, b, zl.at[n]).start()

    def zig_wait(n, src, dst):
        for k in range(2):
            ref = dst.at[pl.ds(k * HALF, HALF)]

            @pl.when(sources[k] != me)
            def _():
                arrived(ref, zs.at[n, 0], zr.at[n, k], {"ctx": sources[k]})

            @pl.when(sources[k] == me)
            def _():
                pltpu.make_async_copy(ref, ref, zl.at[n]).wait()

        for side in range(2):

            @pl.when(owners[side] != me)
            def _():
                a = src.at[pl.ds(side * HALF, HALF)]
                pltpu.make_async_remote_copy(
                    src_ref=a, dst_ref=a, send_sem=zs.at[n, side], recv_sem=zr.at[n, 0],
                    device_id={"ctx": owners[side]}, device_id_type=MESH,
                ).wait_send()

    zig_send(0, result, out_result)
    load.wait()

    def keep(part, index, total):
        own[part] = total

    def e_keep(part, index, total):
        e_sum[index] = total.astype(BF16)

    keys_task = scatter_task(place, dkv, (kh0, kh1, kh2), (kw0, kw1, kw2), ROWS, ks, kr, keep)

    def early():
        yield
        arrived(e_peer, dps.at[0], dpr.at[0], other)
        e_load.wait()
        for part in range(3):
            for z in range(4):
                add_into(e_work, (part, z), e_peer[part, z])
        yield from scatter_task(place, e_work, (eh0, eh1, eh2), (ew0, ew1, ew2), 64, es, er, e_keep)
        yield from gather_task(place, e_sum, 64, gs, gr, lambda phase: None)

    def late():
        yield from keys_task
        cosines, sines = trig[:, 0:HEAD], trig[:, HEAD : 2 * HEAD]
        gain1 = jnp.concatenate([gains[0, 0:1, 0:288], gains[1, 0:1, 0:288]], axis=1)
        keys, values = [], []
        for h in range(KV_HEADS):
            piece = own[h]
            grad_k = piece[:, :HEAD]
            keys.append(grad_k * cosines - swap_halves(grad_k) * sines)
            values.append(piece[:, HEAD:])
        dq_low = dq[...]
        dk_low = jnp.concatenate(keys, axis=1).astype(BF16)
        dv_low = jnp.concatenate(values, axis=1).astype(BF16)
        grads = jnp.concatenate([dq_low, dk_low, dv_low, jnp.zeros((ROWS, 64), BF16)], axis=1)
        weight_grads = tn(h1[...], grads)
        grad_h1 = nt(dq_low, wq[...]) + nt(dk_low, wk[...]) + nt(dv_low, wv[...])
        x = xz[...].astype(F32)
        inverse1 = lax.rsqrt(jnp.mean(x * x, axis=-1, keepdims=True) + EPS)
        grad_norm1, grad_gain1 = rms_backward(x, inverse1, gain1, grad_h1)
        for half in range(2):
            line = jnp.concatenate([grad_gain1[:, 288 * half : 288 * (half + 1)], jnp.zeros((1, 96), F32)], axis=1)
            line = jnp.concatenate([line[:, 128 * k : 128 * (k + 1)] for k in range(3)] + [jnp.zeros((13, 128), F32)], axis=0)
            for chunk in range(192):
                at = (half, chunk // 64, chunk // 16 % 4, chunk // 4 % 4, chunk % 4)
                tile, row = chunk // 18, 288 * half + 16 * (chunk % 18)
                if tile < 8:
                    l_full[at] = weight_grads[row : row + 16, 128 * tile : 128 * (tile + 1)].astype(BF16)
                else:
                    l_full[at] = line.astype(BF16) if chunk == 144 else jnp.zeros((16, 128), BF16)
        l_copy = send(l_full.at[1 - core], l_peer, dps.at[1], dpr.at[1], other)
        grad_z[...] = (dx2[...] + grad_norm1).astype(BF16)
        zig_send(1, grad_z, out_grad)
        yield
        arrived(l_peer, dps.at[1], dpr.at[1], other)
        for part in range(3):
            l_work[part] = (l_full[core, part].astype(F32) + l_peer[part].astype(F32)).astype(BF16)
        yield from small_sum_task(place, l_work, (ls0, ls1, ls2), l_sum, ls, lr, ls2s, ls2r)
        l_copy.wait_send()

    run_together(late(), early())
    e_copy.wait_send()
    zig_wait(0, result, out_result)
    zig_wait(1, grad_z, out_grad)


def end_call(dkv, e, dq, dx2, xz, h1, trig, gains, wq, wk, wv, result):
    def buffers(rows):
        dims = ((4, 4), (4,), ())
        halves = [pltpu.VMEM((3, 2, *d, rows // 2, 128), BF16) for d in dims]
        wholes = [pltpu.VMEM((3, 2, *d, rows, 128), BF16) for d in dims]
        return halves + wholes

    sem = pltpu.SemaphoreType.DMA
    return pl.pallas_call(
        end_kernel,
        out_shape=(
            shape((3, 4, 4, 4, 64, 128), BF16), shape((3, 4, 4, 4, 16, 128), BF16),
            shape((ROWS, D), BF16), shape((ROWS, D), BF16),
        ),
        in_specs=[*anywhere(2), *vmem(10)],
        out_specs=tuple(vmem(4)),
        scratch_shapes=[
            pltpu.VMEM((3, 4, 4, 4, ROWS, 128), BF16),
            pltpu.VMEM((3, 4, 4, 4, 64, 128), BF16), pltpu.VMEM((3, 4, 4, 4, 64, 128), BF16),
            pltpu.VMEM((2, 3, 4, 4, 4, 16, 128), BF16), pltpu.VMEM((3, 4, 4, 4, 16, 128), BF16), pltpu.VMEM((3, 4, 4, 4, 16, 128), BF16),
            pltpu.VMEM((3, ROWS, 128), F32), pltpu.VMEM((ROWS, D), BF16),
            *buffers(ROWS), *buffers(64),
            pltpu.VMEM((3, 3, 4, 4, 16, 128), BF16), pltpu.VMEM((3, 3, 4, 16, 128), BF16), pltpu.VMEM((3, 3, 16, 128), BF16),
            sem((3, 3, 6)), sem((3, 3, 6)), sem((3, 3, 6)), sem((3, 3, 6)), sem((3, 3, 6)), sem((3, 3, 6)),
            sem((3, 3, 3)), sem((3, 3, 3)), sem((3, 3, 3)), sem((3, 3, 3)),
            sem((2,)), sem((2,)), sem((2, 2)), sem((2, 2)), sem((2,)), sem((2,)),
        ],
        compiler_params=pltpu.CompilerParams(collective_id=1, has_side_effects=True, vmem_limit_bytes=VMEM_LIMIT),
        name="reduce_gradients",
    )(dkv, e, dq, dx2, xz, h1, trig, gains, wq, wk, wv, result)


def unpack_kernel(e, l, gain1, gq, gk, gv, go, gain2, gg, gu, gd):
    def take(ref, base, length, out):
        columns = out.shape[1]
        for tile in range(-(-columns // 128)):
            wide = min(128, columns - 128 * tile)
            at = base + tile * length
            out[:, 128 * tile : 128 * tile + wide] = ref[at : at + length, :wide].astype(F32)

    take(e, E_GATE, 288, gg)
    take(e, E_UP, 288, gu)
    take(e, E_DOWN, 768, gd)
    take(e, E_OUT, 288, go)
    gain2[...] = e[E_GAIN : E_GAIN + 16, :].astype(F32)
    gain1[...] = l[8 * 288 : 8 * 288 + 16, :].astype(F32)
    whole = jnp.concatenate([l[tile * 288 : (tile + 1) * 288, :] for tile in range(4, 8)], axis=1).astype(F32)
    take(l, 0, 288, gq)
    gk[...] = whole[:, 64:256]
    gv[...] = whole[:, 256:448]


def unpack_call(e, l):
    return pl.pallas_call(
        unpack_kernel,
        out_shape=(
            shape((16, 128), F32), shape((288, D), F32), shape((288, 192), F32), shape((288, 192), F32),
            shape((288, D), F32), shape((16, 128), F32), shape((288, FF), F32), shape((288, FF), F32), shape((768, D), F32),
        ),
        in_specs=vmem(2),
        out_specs=tuple(vmem(9)),
        compiler_params=pltpu.CompilerParams(vmem_limit_bytes=VMEM_LIMIT),
        name="unpack_gradients",
    )(e, l)


def body(
    layer_in, positions, norm_gain1, w_query, w_key, w_value, w_out, norm_gain2, w_gate, w_up, w_down, cotangent
):
    inv_freq = 10000.0 ** (-jnp.arange(HEAD // 2, dtype=F32) / (HEAD // 2))
    angles = positions[0].astype(F32)[:, None] * inv_freq[None, :]
    cosines, sines = jnp.cos(angles), jnp.sin(angles)
    trig = jnp.concatenate([cosines, cosines, -sines, sines], axis=1)
    gains = jnp.pad(jnp.stack([norm_gain1, norm_gain2]).astype(F32), ((0, 6), (0, 96)))
    xz, trig, cotz, gains, wq, wk, wv, wo, wg, wu, wd, h1, qpad, kv = start_call(
        layer_in[0], trig, cotangent[0], gains, (w_query, w_key, w_value, w_out, w_gate, w_up, w_down)
    )
    wq, wk, wv, wo, wg, wu, wd = (w.reshape(-1, w.shape[-1]) for w in (wq, wk, wv, wo, wg, wu, wd))
    result, e, dkv, dq, dx2 = middle_call(
        xz, cotz, gains, qpad, kv.reshape(KV_HEADS, 64, ROWS, 128), wo, wg, wu, wd, trig
    )
    e_sum, l_sum, result, grad = end_call(
        dkv.reshape(KV_HEADS, 4, 4, 4, ROWS, 128), e.reshape(2, 3, 4, 4, 4, 64, 128),
        dq, dx2, xz, h1, trig, gains, wq, wk, wv, result,
    )
    gain1, gq, gk, gv, go, gain2, gg, gu, gd = unpack_call(e_sum.reshape(-1, 128), l_sum.reshape(-1, 128))
    gain1, gain2 = (g[:3].reshape(-1)[:288] for g in (gain1, gain2))
    return (result[None], grad[None], gain1, gq, gk, gv, go, gain2, gg, gu, gd)


def solution(mesh):
    weight = P("dp", None)
    tokens = P("dp", "ctx", None)
    return jax.shard_map(
        body,
        mesh=mesh,
        in_specs=(tokens, P("dp", "ctx"), P("dp"), weight, weight, weight, weight, P("dp"), weight, weight, weight, tokens),
        out_specs=(tokens, tokens, P("dp"), weight, weight, weight, weight, P("dp"), weight, weight, weight),
        check_vma=False,
    )
```

time: 1060 us -> 292 us (0.28)
  waiting for transfers between devices: 321 us -> 0 us
  Pallas kernels: 0 us -> 274 us
  matrix products: 239 us -> 0 us
  local copies, waits for them, and re-layouts: 204 us -> 14.4 us
  blocking collectives: 186 us -> 0 us
  other arithmetic: 52.2 us -> 2.34 us
  loops' own time: 33.5 us -> 0 us
  between operations: 14.4 us -> 0.67 us
    pallas_call x0 -> x4, Pallas kernels: none -> 274 us  [the longest x1 104 us: start_call(): pl.pallas_call(start_kernel, out_shape=(shape((ROWS, D), BF16), shape((RO...]
    dot_general x133 -> x0, matrix products: 239 us -> none  [the longest x32 47.7 us: masked_scores(): jnp.einsum('tkgd,pkd->kgtp', q_heads, key_block, preferred_element_type=j...]
    reduce_scatter x1 -> x0, waiting for transfers between devices: 212 us -> none  [sent_together(): lax.psum_scatter(both, axis, scatter_dimension=dim, tiled=True)]
    psum x1 -> x0, blocking collectives: 177 us -> none  [body(): lax.psum((shares[0], shares[1], shares[2], shares[3], shares[4], shares[5...]
    dynamic_update_slice x32 -> x0, local copies, waits for them, and re-layouts: 108 us -> none  [the longest x16 54.5 us: step(): lax.dynamic_update_slice_in_dim(grad_k, old_k + part_k, key_start, 0)]
    all_gather x3 -> x0, waiting for transfers between devices: 106 us -> none  [the longest x1 86 us: in_one_piece(): lax.all_gather(both, axis, axis=dim, tiled=True)]
    another operation x2 -> x0, loops' own time: 33.5 us -> none  [key_blocks(): carry, unused = lax.scan(one, carry, (keys, vals, starts))]
    add x84 -> x0, other arithmetic: 21.9 us -> none  [the longest x32 20.7 us: masked_scores(): cols = key_start + jnp.arange(key_block.shape[0], dtype=jnp.int32)]
  transfers between devices with their start and end apart: 6 -> 0, of which waited for: 4 -> 0; matrix products, arithmetic and copies ran while one was open for 11% -> 0% of each run, Pallas kernels for 0% -> 0%
where the time goes in v1:
time: 292 us; the launch traced here: 291 us
  Pallas kernels  274 us (94%)
  local copies, waits for them, and re-layouts  14.4 us (5%)
    pallas_call x1, Pallas kernels, start_call(): pl.pallas_call(start_kernel, out_shape=(shape((ROWS, D), BF16), shape((RO...  104 us
    pallas_call x1, Pallas kernels, end_call(): pl.pallas_call(end_kernel, out_shape=(shape((3, 4, 4, 4, 64, 128), BF16),...  90.9 us
    pallas_call x1, Pallas kernels, middle_call(): pl.pallas_call(middle_kernel, out_shape=(shape((ROWS, D), BF16), shape((2...  73.2 us
    unnamed x6, local copies, waits for them, and re-layouts  11.8 us

profile of v1, /device:TPU:0, one launch (start us, length us, event | category | flops | bytes accessed | tf_op | source)
XLA Modules:
  0.0 291.3 jit_solution(8517391234102049642)
XLA Ops:
  0.6 0.7 convert_bitcast_fusion
  1.3 0.7 stack.9
  2.0 0.7 stack.10
  2.7 0.6 fusion.7.gains_in
  3.3 1.7 copy.29
  5.0 1.7 copy.31
  6.7 0.3 multiply_cosine_fusion
  7.0 0.8 pad_maximum_fusion.trig_in
  7.8 2.2 copy.32.wd_in
  10.0 104.4 %qkv_gather.1 = (bf16[128,576]{1,0:T(8,128)(2,1)}, f32[128,128]{1,0:T(8,128)}, bf16[128,576]{1,0:T(8,128)(2,1)}, f32[2,8,384]{2,1,0:T(8,128)}, bf16[2,288,576]{2...) custom-call(bf16[128,576]{1,0:T(8,128)(2,1)} %bitcast.34, ...), custom_call_target="tpu_custom_call" | custom-call | tf_op jit(solution)/shard_map/qkv_gather/pallas_call | solution.py:376
  114.4 73.2 %attention_and_ffn.1 = (bf16[128,576]{1,0:T(8,128)(2,1)}, bf16[2,12288,128]{2,1,0:T(8,128)(2,1)}, bf16[3,64,128,128]{3,2,1,0:T(8,128)(2,1)}, bf16[128,576]{1,0:T(8,128)(2,1)}, f32[128,576]{1,0:T(8,128)}) custom-call(bf16[128,576]{1,0:T(8,128)(2,1)} %get-tuple-element.43.xz, bf16[128,576]{1,0:T(8,128)(2,1)} %get-tuple-element.44.cotz, ...), custom_call_target="tpu_custom_call" | custom-call | tf_op jit(solution)/shard_map/attention_and_ffn/pallas_call | solution.py:563
  187.6 90.9 %reduce_gradients.1 = (bf16[3,4,4,4,64,128]{5,4,3,2,1,0:T(8,128)(2,1)}, bf16[3,4,4,4,16,128]{5,4,3,2,1,0:T(8,128)(2,1)}, bf16[128,576]{1,0:T(8,128)(2,1)}, bf16[128,576]{1,0:T(8,128)(2,1)}) custom-call(bf16[3,4,4,4,128,128]{5,4,3,2,1,0:T(8,128)(2,1)} %bitcast.26, bf16[2,3,4,4,4,64,128]{6,5,4,3,2,1,0:T(8,128)(2,1)} %bitcast.25, ...), custom_call_target="tpu_custom_call" | custom-call | tf_op jit(solution)/shard_map/reduce_gradients/pallas_call | solution.py:711
  278.6 1.7 copy.33
  280.3 1.7 copy.34
  282.0 5.3 %unpack_gradients.1 = (f32[16,128]{1,0:T(8,128)}, f32[288,576]{1,0:T(8,128)}, f32[288,192]{1,0:T(8,128)}, f32[288,192]{1,0:T(8,128)}, f32[288,576]{1,0:T(8,128)}...) custom-call(bf16[12288,128]{1,0:T(8,128)(2,1)} %bitcast.27, ...), custom_call_target="tpu_custom_call" | custom-call | tf_op jit(solution)/shard_map/unpack_gradients/pallas_call | solution.py:756
  287.3 1.3 slice_bitcast_fusion
  288.6 2.8 copy.35
  (1 shorter events, 0.0 us)

commit v2 on v1

v2 whole, which is shorter than its diff:
```python
import jax
import jax.numpy as jnp
import numpy as np
from jax import lax
from jax.experimental import pallas as pl
from jax.experimental.pallas import tpu as pltpu
from jax.sharding import PartitionSpec as P

HEADS = 9
KV_HEADS = 3
GROUPS = HEADS // KV_HEADS
HEAD = 64
D = 576
FF = 1536
EPS = 1e-05
MASKED = -1e30
HALF = 64
GROUP = 8
KEYS = GROUP * HALF
ROWS = 2 * HALF
MESH = pl.DeviceIdType.MESH
F32 = jnp.float32
BF16 = jnp.bfloat16
VMEM_LIMIT = 60 * 1024 * 1024

E_GATE = 0
E_UP = 12 * 288
E_DOWN = 24 * 288
E_OUT = E_DOWN + 6 * 576
E_GAIN = E_OUT + 5 * 288
E_ROWS = 3 * 64 * 64


def vmem(n):
    return [pl.BlockSpec(memory_space=pltpu.VMEM)] * n


def anywhere(n):
    return [pl.BlockSpec(memory_space=pl.ANY)] * n


def shape(dims, dtype):
    return jax.ShapeDtypeStruct(dims, dtype)


def nn(a, b):
    return jnp.dot(a, b, preferred_element_type=F32)


def nt(a, b):
    return lax.dot_general(a, b, (((1,), (1,)), ((), ())), preferred_element_type=F32)


def tn(a, b):
    return lax.dot_general(a, b, (((0,), (0,)), ((), ())), preferred_element_type=F32)


def run_together(*tasks):
    tasks = list(tasks)
    while tasks:
        for task in list(tasks):
            try:
                next(task)
            except StopIteration:
                tasks.remove(task)


class Place:
    def __init__(self):
        self.core = lax.axis_index("dp")
        self.me = lax.axis_index("ctx")
        self.at = [lax.rem(self.me // 4**a, 4) for a in range(3)]
        self.coords = [[lax.rem(self.at[a] + step, 4) for step in range(4)] for a in range(3)]
        self.devices = [[self.me + (self.coords[a][step] - self.at[a]) * 4**a for step in range(4)] for a in range(3)]

    def toward(self, axis, step):
        return self.devices[axis][step]

    def coord(self, axis, step):
        return self.coords[axis][step]

    def region(self, part, phase, coord):
        index = [None, None, None]
        for k in range(3):
            axis = (part + k) % 3
            index[2 - axis] = pl.ds(0, 4) if k < phase else coord if k == phase else self.at[axis]
        return tuple(index)


def remote(src, dst, send_sem, recv_sem, device):
    return pltpu.make_async_remote_copy(
        src_ref=src, dst_ref=dst, send_sem=send_sem, recv_sem=recv_sem, device_id=device, device_id_type=MESH
    )


def send(src, dst, send_sem, recv_sem, device):
    copy = remote(src, dst, send_sem, recv_sem, device)
    copy.start()
    return copy


class Sends:
    def __init__(self):
        self.made = []

    def start(self, src, src_at, dst, dst_at, send_sem, recv_sem, at, device):
        def make():
            return remote(src.at[src_at], dst.at[dst_at], send_sem.at[at], recv_sem.at[at], device)

        make().start()
        self.made.append(make)

    def wait(self):
        for make in self.made:
            make().wait_send()


def arrived(dst, send_sem, recv_sem, device):
    pltpu.make_async_remote_copy(
        src_ref=dst, dst_ref=dst, send_sem=send_sem, recv_sem=recv_sem, device_id=device, device_id_type=MESH
    ).wait_recv()


def gather_task(place, buf, rows, ssem, rsem, done):
    first, second, whole = pl.ds(0, rows // 2), pl.ds(rows // 2, rows // 2), None
    sent = Sends()
    for phase in range(3):
        for part in range(3):
            axis = (part + phase) % 3
            plus, minus = {"ctx": place.toward(axis, 1)}, {"ctx": place.toward(axis, 3)}
            own = place.region(part, phase, place.at[axis])
            for k, (half, to) in enumerate(((first, plus), (second, minus), (second, plus), (first, minus))):
                index = (part, *own, half)
                sent.start(buf, index, buf, index, ssem, rsem, (part, phase, k), to)
        yield
        for part in range(3):
            axis = (part + phase) % 3
            plus, minus = {"ctx": place.toward(axis, 1)}, {"ctx": place.toward(axis, 3)}
            for k, (half, step, to) in enumerate(((first, 3, plus), (second, 1, minus))):
                index = (part, *place.region(part, phase, place.coord(axis, step)), half)
                arrived(buf.at[index], ssem.at[part, phase, k], rsem.at[part, phase, k], to)
                sent.start(buf, index, buf, index, ssem, rsem, (part, phase, 4 + k), to)
        yield
        for part in range(3):
            axis = (part + phase) % 3
            plus = {"ctx": place.toward(axis, 1)}
            for k, half, step in ((2, second, 3), (3, first, 1), (4, first, 2), (5, second, 2)):
                ref = buf.at[(part, *place.region(part, phase, place.coord(axis, step)), half)]
                arrived(ref, ssem.at[part, phase, k], rsem.at[part, phase, k], plus)
        done(phase)
    yield
    sent.wait()


def add_into(buf, index, other):
    buf[index] = (buf[index].astype(F32) + other.astype(F32)).astype(BF16)


def scatter_task(place, buf, halves, wholes, rows, ssem, rsem, finish):
    first, second = pl.ds(0, rows // 2), pl.ds(rows // 2, rows // 2)
    sent = Sends()
    for turn in range(3):
        phase = 2 - turn
        half_buf, whole_buf = halves[turn], wholes[turn]
        for part in range(3):
            axis = (part + phase) % 3
            plus, minus = {"ctx": place.toward(axis, 1)}, {"ctx": place.toward(axis, 3)}
            far = place.region(part, phase, place.coord(axis, 2))
            right = place.region(part, phase, place.coord(axis, 1))
            left = place.region(part, phase, place.coord(axis, 3))
            lead = (slice(None),) * phase
            for k, src, dst, to in (
                (0, (*far, first), (half_buf, (part, 0)), plus),
                (1, (*far, second), (half_buf, (part, 1)), minus),
                (2, (*right, second), (whole_buf, (part, 0, *lead, second)), plus),
                (3, (*left, first), (whole_buf, (part, 1, *lead, first)), minus),
            ):
                sent.start(buf, (part, *src), *dst, ssem, rsem, (part, turn, k), to)
        yield
        for part in range(3):
            axis = (part + phase) % 3
            plus, minus = {"ctx": place.toward(axis, 1)}, {"ctx": place.toward(axis, 3)}
            lead = (slice(None),) * phase
            for k, half, step, to in ((0, first, 1, plus), (1, second, 3, minus)):
                arrived(half_buf.at[part, k], ssem.at[part, turn, k], rsem.at[part, turn, k], to)
                index = (part, *place.region(part, phase, place.coord(axis, step)), half)
                add_into(buf, index, half_buf[part, k])
                sent.start(buf, index, whole_buf, (part, k, *lead, half), ssem, rsem, (part, turn, 4 + k), to)
        yield
        for part in range(3):
            axis = (part + phase) % 3
            plus = {"ctx": place.toward(axis, 1)}
            lead = (slice(None),) * phase
            for k, side, half in ((2, 0, second), (3, 1, first), (4, 0, first), (5, 1, second)):
                dst = whole_buf.at[(part, side, *lead, half)]
                arrived(dst, ssem.at[part, turn, k], rsem.at[part, turn, k], plus)
            index = (part, *place.region(part, phase, place.at[axis]))
            total = buf[index].astype(F32) + whole_buf[part, 0].astype(F32) + whole_buf[part, 1].astype(F32)
            if turn < 2:
                buf[index] = total.astype(BF16)
            else:
                finish(part, index, total)
    yield
    sent.wait()


def small_sum_task(place, buf, slots, out, ssem, rsem, ssem2, rsem2):
    sent = Sends()
    for turn in range(3):
        phase = 2 - turn
        for part in range(3):
            axis = (part + phase) % 3
            for k in range(3):
                index = (part, *place.region(part, phase, place.coord(axis, k + 1)))
                to = {"ctx": place.toward(axis, k + 1)}
                sent.start(buf, index, slots[turn], (part, k), ssem, rsem, (part, turn, k), to)
        yield
        for part in range(3):
            axis = (part + phase) % 3
            index = (part, *place.region(part, phase, place.at[axis]))
            total = buf[index].astype(F32)
            for k in range(3):
                to = {"ctx": place.toward(axis, k + 1)}
                arrived(slots[turn].at[part, k], ssem.at[part, turn, k], rsem.at[part, turn, k], to)
                total = total + slots[turn][part, k].astype(F32)
            if turn < 2:
                buf[index] = total.astype(BF16)
            else:
                out[index] = total.astype(BF16)
    for phase in range(3):
        for part in range(3):
            axis = (part + phase) % 3
            index = (part, *place.region(part, phase, place.at[axis]))
            for k in range(3):
                to = {"ctx": place.toward(axis, k + 1)}
                sent.start(out, index, out, index, ssem2, rsem2, (part, phase, k), to)
        yield
        for part in range(3):
            axis = (part + phase) % 3
            for k in range(3):
                to = {"ctx": place.toward(axis, k + 1)}
                ref = out.at[(part, *place.region(part, phase, place.coord(axis, 3 - k)))]
                arrived(ref, ssem2.at[part, phase, k], rsem2.at[part, phase, k], to)
    yield
    sent.wait()


def greet(place, partners):
    barrier = pltpu.get_barrier_semaphore()
    for axis in range(3):
        for step in (1, 2, 3):
            pl.semaphore_signal(barrier, inc=1, device_id={"ctx": place.toward(axis, step)}, device_id_type=MESH)
    pl.semaphore_signal(barrier, inc=1, device_id={"dp": 1 - place.core}, device_id_type=MESH)
    count = 10
    for partner in partners:

        @pl.when(partner != place.me)
        def _():
            pl.semaphore_signal(barrier, inc=1, device_id={"ctx": partner}, device_id_type=MESH)

        count = count + jnp.where(partner != place.me, 1, 0)
    pl.semaphore_wait(barrier, count)


def folded(half_block):
    return jnp.where(half_block < 64, half_block, 127 - half_block)


def swap_halves(v):
    return jnp.concatenate([v[:, HEAD // 2 :], v[:, : HEAD // 2]], axis=1)


def rms_forward(values, gain):
    inverse = lax.rsqrt(jnp.mean(values * values, axis=-1, keepdims=True) + EPS)
    return values * inverse * gain, inverse


def rms_backward(values, inverse, gain, grad):
    normal = values * inverse
    grad_gain = jnp.sum(grad * normal, axis=0, keepdims=True)
    scaled = grad * gain
    grad_in = inverse * (scaled - normal * jnp.mean(scaled * normal, axis=-1, keepdims=True))
    return grad_in, grad_gain


def layer_kernel(
    x_in, trig_in, cot_in, gain1_in, gain2_in, wq_in, wk_in, wv_in, wo_in, wg_in, wu_in, wd_in,
    e_sum, l_sum, out_result, out_grad,
    x_rows, cot_rows, g_rows, xz, trig, cotz, gains, wq, wk, wv, wo, wg, wu, wd, h1_kept, qpad, kv,
    outs_t, lse, dopad, attn, dq_early, dq_late, dq_rows, result, grad_x2_kept,
    dkv, e_all, e_peer, l_full, l_peer, l_work, own, grad_z,
    kh0, kh1, kh2, kw0, kw1, kw2, eh0, eh1, eh2, ew0, ew1, ew2, ls0, ls1, ls2,
    in_send, in_recv, in_local, dp_send, dp_recv, dp_local, as_, ar,
    ks, kr, es, er, gs, gr, ls, lr, ls2s, ls2r, dps, dpr, zs, zr, zl,
):
    place = Place()
    me, core = place.me, place.core
    every = range(KV_HEADS)

    x_rows[...] = x_in[...].T
    g_rows[...] = jnp.zeros((8, 384), F32)
    g_rows[0:1, 0:288] = gain1_in[...].astype(F32).reshape(1, 288)
    g_rows[1:2, 0:288] = gain2_in[...].astype(F32).reshape(1, 288)
    cot_rows[...] = cot_in[...].T
    targets = [folded(2 * me + k) for k in range(2)]
    owners = [me // 2, (127 - me) // 2]
    greet(place, owners + targets)
    slot = me // 32
    moved = ((x_rows, xz), (trig_in, trig), (cot_rows, cotz))

    def in_copy(n, k, here=False):
        src, dst = moved[n]
        a, b = src.at[pl.ds(HALF * k, HALF)], dst.at[pl.ds(pl.multiple_of(slot * HALF, HALF), HALF)]
        if here:
            return pltpu.make_async_copy(a, b, in_local.at[n])
        return remote(a, b, in_send.at[n, k], in_recv.at[n, slot], {"ctx": targets[k]})

    for n in range(3):
        for k in range(2):

            @pl.when(targets[k] != me)
            def _():
                in_copy(n, k).start()

            @pl.when(targets[k] == me)
            def _():
                in_copy(n, k, here=True).start()

    other = {"dp": 1 - core}
    weights = ((g_rows, gains), (wq_in, wq), (wk_in, wk), (wv_in, wv), (wo_in, wo), (wg_in, wg), (wu_in, wu), (wd_in, wd))
    copies = []
    for n, (src, dst) in enumerate(weights):
        there = send(src, dst.at[core], dp_send.at[n], dp_recv.at[n], other)
        here = pltpu.make_async_copy(src, dst.at[core], dp_local.at[n])
        here.start()
        copies.append((there, here))

    def in_wait(n):
        dst = moved[n][1]
        for side in range(2):
            ref = dst.at[pl.ds(side * HALF, HALF)]

            @pl.when(owners[side] != me)
            def _():
                arrived(ref, in_send.at[n, 0], in_recv.at[n, side], {"ctx": owners[side]})

            @pl.when(owners[side] == me)
            def _():
                pltpu.make_async_copy(ref, ref, in_local.at[n]).wait()

    def dp_wait(n):
        copies[n][1].wait()
        arrived(weights[n][1].at[1 - core], dp_send.at[n], dp_recv.at[n], other)

    in_wait(0)
    in_wait(1)
    dp_wait(0)
    gain1 = jnp.concatenate([gains[0, 0:1, 0:288], gains[1, 0:1, 0:288]], axis=1)
    gain2 = jnp.concatenate([gains[0, 1:2, 0:288], gains[1, 1:2, 0:288]], axis=1)
    x = xz[...].astype(F32)
    h1f, _ = rms_forward(x, gain1)
    h1 = h1f.astype(BF16)
    h1_kept[...] = h1
    for n in (1, 2, 3):
        dp_wait(n)

    def whole(ref):
        return ref[...].reshape(D, ref.shape[-1])

    cosines, sines = trig[:, 0:HEAD], trig[:, HEAD : 2 * HEAD]
    k_lin = nn(h1, whole(wk))
    v_lin = nn(h1, whole(wv))
    for h in every:
        cols = slice(h * HEAD, (h + 1) * HEAD)
        key = k_lin[:, cols]
        key = key * cosines + swap_halves(key) * sines
        kv[h, place.at[2], place.at[1], place.at[0]] = jnp.concatenate([key, v_lin[:, cols]], axis=1).astype(BF16)
    task = gather_task(place, kv, ROWS, as_, ar, lambda phase: None)
    next(task)
    q_lin = nn(h1, whole(wq))
    for h in range(HEADS):
        query = q_lin[:, h * HEAD : (h + 1) * HEAD]
        query = (query * cosines + swap_halves(query) * sines).astype(BF16)
        query = (query.astype(F32) * HEAD**-0.5).astype(BF16)
        query = jnp.concatenate([query, jnp.zeros((ROWS, HEAD), BF16)], axis=1)
        group = (h % GROUPS) * HALF
        qpad[h // GROUPS, group : group + HALF] = query[:HALF]
        qpad[h // GROUPS, 192 + group : 192 + group + HALF] = query[HALF:]
    run_together(task)
    in_wait(2)
    for n in (4, 5, 6, 7):
        dp_wait(n)

    mine = me // GROUP
    within = lax.rem(me, GROUP)
    key_row = lax.broadcasted_iota(jnp.int32, (KEYS, 384), 0)
    lane = lax.broadcasted_iota(jnp.int32, (KEYS, 384), 1)
    low_mask = key_row <= jnp.where(lane < 192, HALF * within + lax.rem(lane, HALF), KEYS)
    key_row = key_row[:, :192]
    lane = lane[:, :192]
    high_mask = lax.rem(key_row, HALF) - HALF * (key_row // HALF) <= lax.rem(lane, HALF) - HALF * within

    def keys_of(h, g, side):
        return kv[h, g // 2, pl.ds(2 * lax.rem(g, 2), 2), :, side * HALF : (side + 1) * HALF, :].reshape(KEYS, 128)

    def keys_both(h, g):
        return jnp.concatenate([keys_of(h, g, 0), keys_of(h, g, 1)], axis=0)

    def forward_step(block, queries, mask, state):
        top, accum = state
        scores = nt(block, queries)
        if mask is not None:
            scores = jnp.where(mask, scores, MASKED)
        new_top = jnp.maximum(top, jnp.max(scores, axis=0, keepdims=True))
        weights = jnp.exp(scores - new_top).astype(BF16)
        ones_lane = lax.broadcasted_iota(jnp.int32, block.shape, 1) < HEAD
        values = jnp.where(ones_lane, jnp.ones_like(block), block)
        return new_top, accum * jnp.exp(top - new_top) + tn(values, weights)

    late_rows = slice(192, 384)
    state = [(jnp.full((1, 384), MASKED, F32), jnp.zeros((128, 384), F32)) for h in every]
    state = lax.fori_loop(
        0, mine, lambda g, s: [forward_step(keys_of(h, g, 0), qpad[h], None, s[h]) for h in every], state
    )
    state = [forward_step(keys_of(h, mine, 0), qpad[h], low_mask, state[h]) for h in every]
    late = [
        forward_step(keys_of(h, mine, 1), qpad[h, late_rows], high_mask, (state[h][0][:, 192:], state[h][1][:, 192:]))
        for h in every
    ]
    late = lax.fori_loop(
        mine + 1, 8, lambda g, s: [forward_step(keys_both(h, g), qpad[h, late_rows], None, s[h]) for h in every], late
    )
    for h in every:
        top = jnp.concatenate([state[h][0][:, :192], late[h][0]], axis=1)
        accum = jnp.concatenate([state[h][1][:, :192], late[h][1]], axis=1)
        total = accum[0:1, :]
        outs = accum / total
        outs_t[h] = outs
        lse[h] = top + jnp.log(total)
        attn[h] = outs.T.astype(BF16)

    def by_token(ref, lanes):
        pieces = []
        for h in range(HEADS):
            group = (h % GROUPS) * HALF
            here = ref[h // GROUPS]
            pieces.append(jnp.concatenate([here[group : group + HALF, lanes], here[192 + group : 192 + group + HALF, lanes]], axis=0))
        return jnp.concatenate(pieces, axis=1)

    attn_low = by_token(attn, slice(64, 128))

    def put(base, length, value, half):
        for tile in range(value.shape[1] // 128):
            at, done = base + tile * length, 0
            while done < value.shape[0]:
                chunk, row = (at + done) // 64, (at + done) % 64
                size = min(64 - row, value.shape[0] - done)
                spot = (half, chunk // 64, chunk // 16 % 4, chunk // 4 % 4, chunk % 4, slice(row, row + size))
                e_all[spot] = value[done : done + size, tile * 128 : (tile + 1) * 128].astype(BF16)
                done += size

    def gain_line(grad, half):
        line = jnp.concatenate([grad[:, 288 * half : 288 * (half + 1)], jnp.zeros((1, 96), F32)], axis=1)
        return jnp.concatenate([line[:, 128 * k : 128 * (k + 1)] for k in range(3)] + [jnp.zeros((13, 128), F32)], axis=0)

    x2 = x + nn(attn_low, whole(wo))
    h2f, inverse2 = rms_forward(x2, gain2)
    h2 = h2f.astype(BF16)
    pad = jnp.zeros((ROWS, 64), BF16)
    dy_low = cotz[...]
    total = x2
    grad_h2 = jnp.zeros((ROWS, D), F32)
    for t in range(2):
        cols = slice(768 * t, 768 * (t + 1))
        wg_t, wu_t = wg[:, :, cols].reshape(D, 768), wu[:, :, cols].reshape(D, 768)
        gate = nn(h2, wg_t)
        up = nn(h2, wu_t)
        sigma = jax.nn.sigmoid(gate)
        active = gate * sigma
        hidden = (active * up).astype(BF16)
        total = total + nt(hidden, wd[t])
        grad_hidden = nn(dy_low, wd[t])
        grad_gate = (grad_hidden * up * (sigma + active * (1.0 - sigma))).astype(BF16)
        grad_up = (grad_hidden * active).astype(BF16)
        grad_h2 = grad_h2 + nt(grad_gate, wg_t) + nt(grad_up, wu_t)
        for base, value in ((E_GATE, tn(h2, grad_gate)), (E_UP, tn(h2, grad_up))):
            for half in range(2):
                put(base + 6 * t * 288, 288, value[288 * half : 288 * (half + 1)], half)
        put(E_DOWN, 576, tn(dy_low, hidden), t)
    result[...] = total.astype(BF16)
    grad_norm2, grad_gain2 = rms_backward(x2, inverse2, gain2, grad_h2)
    grad_x2 = dy_low.astype(F32) + grad_norm2
    grad_x2_kept[...] = grad_x2
    grad_attn = grad_x2.astype(BF16)
    grad_out = tn(attn_low, jnp.concatenate([grad_attn, pad], axis=1))
    for half in range(2):
        put(E_OUT, 288, grad_out[288 * half : 288 * (half + 1)], half)
        put(E_GAIN, 16, gain_line(grad_gain2, half), half)
        put(E_GAIN + 16, 0, jnp.zeros((E_ROWS - E_GAIN - 16, 128), F32), half)
    send(e_all.at[1 - core], e_peer, dps.at[0], dpr.at[0], other)

    def out_copy(n, side, here=False):
        src, dst = ((result, out_result), (grad_z, out_grad))[n]
        k = lax.rem((me, 127 - me)[side], 2)
        a = src.at[pl.ds(side * HALF, HALF)]
        b = dst.at[pl.ds(pl.multiple_of(k * HALF, HALF), HALF)]
        if here:
            return pltpu.make_async_copy(a, b, zl.at[n])
        return remote(a, b, zs.at[n, side], zr.at[n, k], {"ctx": owners[side]})

    def out_send(n):
        for side in range(2):

            @pl.when(owners[side] != me)
            def _():
                out_copy(n, side).start()

            @pl.when(owners[side] == me)
            def _():
                out_copy(n, side, here=True).start()

    def out_wait(n):
        dst = (out_result, out_grad)[n]
        for k in range(2):
            ref = dst.at[pl.ds(k * HALF, HALF)]

            @pl.when(targets[k] != me)
            def _():
                arrived(ref, zs.at[n, 0], zr.at[n, k], {"ctx": targets[k]})

            @pl.when(targets[k] == me)
            def _():
                pltpu.make_async_copy(ref, ref, zl.at[n]).wait()

        for side in range(2):

            @pl.when(owners[side] != me)
            def _():
                out_copy(n, side).wait_send()

    out_send(0)
    e_work = e_all.at[core]

    def early():
        arrived(e_peer, dps.at[0], dpr.at[0], other)
        remote(e_all.at[1 - core], e_peer, dps.at[0], dpr.at[0], other).wait_send()
        for part in range(3):
            for z in range(4):
                index = (core, part, z)
                e_all[index] = (e_all[index].astype(F32) + e_peer[part, z].astype(F32)).astype(BF16)

        def e_keep(part, index, total):
            e_sum[index] = total.astype(BF16)

        yield from scatter_task(place, e_work, (eh0, eh1, eh2), (ew0, ew1, ew2), 64, es, er, e_keep)
        yield from gather_task(place, e_sum, 64, gs, gr, lambda phase: None)

    early_task = early()

    grad_o = nt(grad_attn, whole(wo)).astype(BF16)
    for h in range(HEADS):
        piece = grad_o[:, h * HEAD : (h + 1) * HEAD]
        piece = jnp.concatenate([jnp.zeros((ROWS, HEAD), BF16), piece], axis=1)
        group = (h % GROUPS) * HALF
        dopad[h // GROUPS, group : group + HALF] = piece[:HALF]
        dopad[h // GROUPS, 192 + group : 192 + group + HALF] = piece[HALF:]

    deltas = [jnp.sum(dopad[h].astype(F32).T * outs_t[h], axis=0, keepdims=True) for h in every]
    logs = [lse[h] for h in every]

    def backward_step(block, queries, grads, log_total, delta, mask, grad_q):
        scores = nt(block, queries)
        if mask is not None:
            scores = jnp.where(mask, scores, MASKED)
        probs = jnp.exp(scores - log_total)
        grad_scores = (probs * (nt(block, grads) - delta)).astype(BF16)
        part = nn(grad_scores, queries) + nn(probs.astype(BF16), grads)
        return grad_q + tn(block, grad_scores), part.astype(BF16)

    def save(h, g, side, part):
        spot = (h, g // 2, pl.ds(2 * lax.rem(g, 2), 2), slice(None), slice(side * HALF, (side + 1) * HALF))
        dkv[spot] = part.reshape(2, 4, HALF, 128)

    dq_early[...] = jnp.zeros_like(dq_early)
    dq_late[...] = jnp.zeros_like(dq_late)

    def early_keys(g, mask):
        for h in every:
            dq_early[h], part = backward_step(
                keys_of(h, g, 0), qpad[h], dopad[h], logs[h], deltas[h], mask, dq_early[h]
            )
            save(h, g, 0, part)

    def late_keys(block_of, g, mask):
        parts = []
        for h in every:
            dq_late[h], part = backward_step(
                block_of(h, g), qpad[h, late_rows], dopad[h, late_rows], logs[h][:, 192:], deltas[h][:, 192:],
                mask, dq_late[h],
            )
            parts.append(part)
        return parts

    def backward(g, _):
        for k in range(8):

            @pl.when(g == k)
            def _():
                next(early_task)

        @pl.when(g < mine)
        def _():
            early_keys(g, None)
            for h in every:
                save(h, g, 1, jnp.zeros((KEYS, 128), BF16))

        @pl.when(g == mine)
        def _():
            early_keys(g, low_mask)
            for h, part in enumerate(late_keys(lambda h, g: keys_of(h, g, 1), g, high_mask)):
                save(h, g, 1, part)

        @pl.when(g > mine)
        def _():
            for h, part in enumerate(late_keys(keys_both, g, None)):
                save(h, g, 0, part[:KEYS])
                save(h, g, 1, part[KEYS:])

        return 0

    lax.fori_loop(0, 8, backward, 0)

    def keep(part, index, total):
        own[part] = total

    keys_task = scatter_task(place, dkv, (kh0, kh1, kh2), (kw0, kw1, kw2), ROWS, ks, kr, keep)

    def late_part():
        next(keys_task)
        for h in every:
            dq_rows[h] = jnp.concatenate([dq_early[h][:, :192], dq_early[h][:, 192:] + dq_late[h]], axis=1).T
        grad_q = by_token(dq_rows, slice(0, 64)) * HEAD**-0.5
        pieces = []
        for h in range(HEADS):
            piece = grad_q[:, h * HEAD : (h + 1) * HEAD]
            pieces.append(piece * cosines - swap_halves(piece) * sines)
        dq_low = jnp.concatenate(pieces, axis=1).astype(BF16)
        grad_h1 = nt(dq_low, whole(wq))
        yield from keys_task
        keys, values = [], []
        for h in every:
            piece = own[h]
            grad_k = piece[:, :HEAD]
            keys.append(grad_k * cosines - swap_halves(grad_k) * sines)
            values.append(piece[:, HEAD:])
        dk_low = jnp.concatenate(keys, axis=1).astype(BF16)
        dv_low = jnp.concatenate(values, axis=1).astype(BF16)
        grads = jnp.concatenate([dq_low, dk_low, dv_low, jnp.zeros((ROWS, 64), BF16)], axis=1)
        weight_grads = tn(h1_kept[...], grads)
        grad_h1 = grad_h1 + nt(dk_low, whole(wk)) + nt(dv_low, whole(wv))
        x = xz[...].astype(F32)
        inverse1 = lax.rsqrt(jnp.mean(x * x, axis=-1, keepdims=True) + EPS)
        grad_norm1, grad_gain1 = rms_backward(x, inverse1, gain1, grad_h1)
        for half in range(2):
            line = gain_line(grad_gain1, half).astype(BF16)
            for chunk in range(192):
                at = (half, chunk // 64, chunk // 16 % 4, chunk // 4 % 4, chunk % 4)
                tile, row = chunk // 18, 288 * half + 16 * (chunk % 18)
                if tile < 8:
                    l_full[at] = weight_grads[row : row + 16, 128 * tile : 128 * (tile + 1)].astype(BF16)
                else:
                    l_full[at] = line if chunk == 144 else jnp.zeros((16, 128), BF16)
        l_copy = send(l_full.at[1 - core], l_peer, dps.at[1], dpr.at[1], other)
        grad_z[...] = (grad_x2_kept[...] + grad_norm1).astype(BF16)
        out_send(1)
        yield
        arrived(l_peer, dps.at[1], dpr.at[1], other)
        for part in range(3):
            l_work[part] = (l_full[core, part].astype(F32) + l_peer[part].astype(F32)).astype(BF16)
        yield from small_sum_task(place, l_work, (ls0, ls1, ls2), l_sum, ls, lr, ls2s, ls2r)
        l_copy.wait_send()

    run_together(late_part(), early_task)
    out_wait(0)
    out_wait(1)
    for there, _ in copies:
        there.wait_send()
    for n in range(3):
        for k in range(2):

            @pl.when(targets[k] != me)
            def _():
                in_copy(n, k).wait_send()


def layer_call(x, trig, cot, gain1, gain2, weights):
    def buffers(rows):
        dims = ((4, 4), (4,), ())
        halves = [pltpu.VMEM((3, 2, *d, rows // 2, 128), BF16) for d in dims]
        wholes = [pltpu.VMEM((3, 2, *d, rows, 128), BF16) for d in dims]
        return halves + wholes

    sem = pltpu.SemaphoreType.DMA
    v = pltpu.VMEM
    return pl.pallas_call(
        layer_kernel,
        out_shape=(
            shape((3, 4, 4, 4, 64, 128), BF16), shape((3, 4, 4, 4, 16, 128), BF16),
            shape((ROWS, D), BF16), shape((ROWS, D), BF16),
        ),
        in_specs=(*vmem(5), *anywhere(7)),
        out_specs=tuple(vmem(4)),
        scratch_shapes=[
            v((ROWS, D), BF16), v((ROWS, D), BF16), v((8, 384), F32),
            v((ROWS, D), BF16), v((ROWS, 128), F32), v((ROWS, D), BF16), v((2, 8, 384), F32),
            *[v((2, *w.shape), BF16) for w in weights],
            v((ROWS, D), BF16), v((KV_HEADS, 384, 128), BF16), v((KV_HEADS, 4, 4, 4, ROWS, 128), BF16),
            v((KV_HEADS, 128, 384), F32), v((KV_HEADS, 1, 384), F32), v((KV_HEADS, 384, 128), BF16),
            v((KV_HEADS, 384, 128), BF16), v((KV_HEADS, 128, 384), F32), v((KV_HEADS, 128, 192), F32),
            v((KV_HEADS, 384, 128), F32), v((ROWS, D), BF16), v((ROWS, D), F32),
            v((3, 4, 4, 4, ROWS, 128), BF16), v((2, 3, 4, 4, 4, 64, 128), BF16), v((3, 4, 4, 4, 64, 128), BF16),
            v((2, 3, 4, 4, 4, 16, 128), BF16), v((3, 4, 4, 4, 16, 128), BF16), v((3, 4, 4, 4, 16, 128), BF16),
            v((3, ROWS, 128), F32), v((ROWS, D), BF16),
            *buffers(ROWS), *buffers(64),
            v((3, 3, 4, 4, 16, 128), BF16), v((3, 3, 4, 16, 128), BF16), v((3, 3, 16, 128), BF16),
            sem((3, 2)), sem((3, 2)), sem((3,)), sem((8,)), sem((8,)), sem((8,)), sem((3, 3, 6)), sem((3, 3, 6)),
            sem((3, 3, 6)), sem((3, 3, 6)), sem((3, 3, 6)), sem((3, 3, 6)), sem((3, 3, 6)), sem((3, 3, 6)),
            sem((3, 3, 3)), sem((3, 3, 3)), sem((3, 3, 3)), sem((3, 3, 3)),
            sem((2,)), sem((2,)), sem((2, 2)), sem((2, 2)), sem((2,)),
        ],
        compiler_params=pltpu.CompilerParams(collective_id=0, has_side_effects=True, vmem_limit_bytes=VMEM_LIMIT),
        name="decoder_layer",
    )(x, trig, cot, gain1, gain2, *weights)


def unpack_kernel(e, l, result, grad, result_t, grad_t, gain1, gq, gk, gv, go, gain2, gg, gu, gd):
    def take(ref, base, length, out):
        columns = out.shape[1]
        for tile in range(-(-columns // 128)):
            wide = min(128, columns - 128 * tile)
            at = base + tile * length
            out[:, 128 * tile : 128 * tile + wide] = ref[at : at + length, :wide].astype(F32)

    take(e, E_GATE, 288, gg)
    take(e, E_UP, 288, gu)
    take(e, E_DOWN, 576, gd)
    result_t[...] = result[...].T
    grad_t[...] = grad[...].T
    take(e, E_OUT, 288, go)
    gain2[...] = e[E_GAIN : E_GAIN + 16, :].astype(F32)
    gain1[...] = l[8 * 288 : 8 * 288 + 16, :].astype(F32)
    whole = jnp.concatenate([l[tile * 288 : (tile + 1) * 288, :] for tile in range(4, 8)], axis=1).astype(F32)
    take(l, 0, 288, gq)
    gk[...] = whole[:, 64:256]
    gv[...] = whole[:, 256:448]


def unpack_call(e, l, result, grad):
    return pl.pallas_call(
        unpack_kernel,
        out_shape=(
            shape((D, ROWS), BF16), shape((D, ROWS), BF16),
            shape((16, 128), F32), shape((288, D), F32), shape((288, 192), F32), shape((288, 192), F32),
            shape((288, D), F32), shape((16, 128), F32), shape((288, FF), F32), shape((288, FF), F32), shape((D, 768), F32),
        ),
        in_specs=vmem(4),
        out_specs=tuple(vmem(11)),
        compiler_params=pltpu.CompilerParams(vmem_limit_bytes=VMEM_LIMIT),
        name="unpack_gradients",
    )(e, l, result, grad)


def body(
    layer_in, positions, norm_gain1, w_query, w_key, w_value, w_out, norm_gain2, w_gate, w_up, w_down, cotangent
):
    inv_freq = np.tile(10000.0 ** (-np.arange(HEAD // 2) / (HEAD // 2)), 4).astype(np.float32)
    angles = positions[0].astype(F32)[:, None] * inv_freq[None, :]
    lane = lax.broadcasted_iota(jnp.int32, (ROWS, 128), 1)
    sines = jnp.sin(angles)
    trig = jnp.where(lane < 64, jnp.cos(angles), jnp.where(lane < 96, -sines, sines))
    e_sum, l_sum, result, grad = layer_call(
        layer_in[0].T, trig, cotangent[0].T, norm_gain1, norm_gain2,
        (w_query, w_key, w_value, w_out, w_gate, w_up, w_down.T),
    )
    result, grad, gain1, gq, gk, gv, go, gain2, gg, gu, gd = unpack_call(
        e_sum.reshape(-1, 128), l_sum.reshape(-1, 128), result, grad
    )
    gain1, gain2 = (g[:3].reshape(-1)[:288] for g in (gain1, gain2))
    return (result.T[None], grad.T[None], gain1, gq, gk, gv, go, gain2, gg, gu, gd.T)


def solution(mesh):
    weight = P("dp", None)
    tokens = P("dp", "ctx", None)
    return jax.shard_map(
        body,
        mesh=mesh,
        in_specs=(tokens, P("dp", "ctx"), P("dp"), weight, weight, weight, weight, P("dp"), weight, weight, weight, tokens),
        out_specs=(tokens, tokens, P("dp"), weight, weight, weight, weight, P("dp"), weight, weight, weight),
        check_vma=False,
    )
```

time: 292 us -> 192 us (0.66)
  Pallas kernels: 274 us -> 187 us
  local copies, waits for them, and re-layouts: 14.4 us -> 2.51 us
    pallas_call x4 -> x2, Pallas kernels: 274 us -> 187 us  [the longest x1 181 us: layer_call(): pl.pallas_call(layer_kernel, out_shape=(shape((3, 4, 4, 4, 64, 128), BF16...]
    unnamed x6 -> x0, local copies, waits for them, and re-layouts: 11.8 us -> none
where the time goes in v2:
time: 192 us
  Pallas kernels  187 us (97%)
  local copies, waits for them, and re-layouts  2.51 us (1%)
  other arithmetic  2.27 us (1%)
    pallas_call x1, Pallas kernels, layer_call(): pl.pallas_call(layer_kernel, out_shape=(shape((3, 4, 4, 4, 64, 128), BF16...  181 us
    pallas_call x1, Pallas kernels, unpack_call(): pl.pallas_call(unpack_kernel, out_shape=(shape((D, ROWS), BF16), shape((D...  5.46 us

profile of v2, /device:TPU:0, one launch (start us, length us, event | category | flops | bytes accessed | tf_op | source)
XLA Modules:
  0.0 192.3 jit_solution(3757080672217183421)
XLA Ops:
  0.6 0.7 convert_bitcast_fusion
  1.3 1.6 fusion.trig_in
  2.9 181.4 %decoder_layer.1 = (bf16[3,4,4,4,64,128]{5,4,3,2,1,0:T(8,128)(2,1)}, bf16[3,4,4,4,16,128]{5,4,3,2,1,0:T(8,128)(2,1)}, bf16[128,576]{1,0:T(8,128)(2,1)}, bf16[128,576]{1,0:T(8,128)(2,1)}) custom-call(bf16[576,128]{1,0:T(8,128)(2,1)} %bitcast.27, f32[128,128]{1,0:T(8,128)} %fusion.trig_in, bf16[576,128]{1,0:T(8,128)(2,1)} %bitcast.28, bf16[288]{0:T(512)(128)(2,1)} %gain1_in.1, ...), custom_call_target="tpu_custom_call" | custom-call | tf_op jit(solution)/shard_map/decoder_layer/pallas_call | solution.py:705
  184.3 5.5 %unpack_gradients.1 = (bf16[576,128]{1,0:T(8,128)(2,1)}, bf16[576,128]{1,0:T(8,128)(2,1)}, f32[16,128]{1,0:T(8,128)}, f32[288,576]{1,0:T(8,128)}, f32[288,192]{1...) custom-call(bf16[12288,128]{1,0:T(8,128)(2,1)} %bitcast.24, ...), custom_call_target="tpu_custom_call" | custom-call | tf_op jit(solution)/shard_map/unpack_gradients/pallas_call | solution.py:759
  189.7 1.3 slice_bitcast_fusion.1
  191.0 1.3 slice_bitcast_fusion
  (1 shorter events, 0.0 us)
